TPU v7x, 32 devices: a whole 2x2x4 slice. The times are simulated.
32 devices in a mesh: spin: 4 (over y, core), fock: 8 (over z, x).
Axes of the slice: x: 2, y: 2, z: 4, core: 2. Of those that a mesh axis runs over, the one named last changes fastest.
Arguments:
- amplitudes: float32 [2, 8192, 8192], P(None, 'spin', 'fock'), may hold values from -6 to 6
- cutoffs: int32 [8192], P('spin'), may hold values from 256 to 512
- coupling_first: float32 [13], replicated, may hold values from 0.05 to 0.5
- coupling_second: float32 [13], replicated, may hold values from 0.2 to 2
- frozen_coupling: float32 [16], replicated, may hold values from 1 to 4
- frozen_bits: int32 [16], replicated, may hold values from 0 to 1, as said below
- drive_bits: int32 [13], replicated, may hold values 0 or 1
- angles: float32 [13], replicated, may hold values from 0.3 to 1.3
Outputs:
- evolved: float32 [2, 8192, 8192], P(None, 'spin', 'fock')
Inputs may be any that keep to these rules, and one draw needn't show every extreme that they name: `cutoffs`: highest level plus one of the first mode that the ladder couples in each spin configuration. `frozen_bits`: between one and four frozen spins have bit 1, the others bit 0.
All inputs are finite; a program needn't handle non-finite values.
Results may differ from a plain program's by a relative error of at most 0.0003.
Values sent between devices are 32-bit elements; how exact they have to be, the bound alone decides.
No kernel may reach another device: no remote copies, remote signals or barrier semaphores. Data moves between devices by JAX's collectives and lax.ppermute only.
A program may use at most 256 MiB of HBM per device.

v0:
```python
import math

import jax
import jax.numpy as jnp
from jax import lax
from jax.sharding import PartitionSpec as P

SPINS = 13
FA = 512
FB = 16
DEGREE = 16


evolve_time = 12.0
diagonal_first = 0.06
diagonal_second = 0.04
ladder_first = 0.35
ladder_second = 0.1


def extended(value, sides, width):
    for axis, dim in sides:
        size, length = (lax.axis_size(axis), value.shape[dim])
        up = [(i, (i + 1) % size) for i in range(size - 1)]
        down = [(j, i) for i, j in up]
        last = lax.slice_in_dim(value, length - width, length, axis=dim)
        initial = lax.slice_in_dim(value, 0, width, axis=dim)
        before = lax.ppermute(last, axis, up)
        after = lax.ppermute(initial, axis, down)
        value = jnp.concatenate([before, value, after], axis=dim)
    return value


def bessel_first(term_order, argument):
    running = 0.0
    addend = (argument / 2.0) ** term_order / math.factorial(term_order)
    for serial in range(80):
        running = running + addend
        addend = addend * -(argument * argument / 4.0) / ((serial + 1) * (serial + 1 + term_order))
    return running


def coefficient_table(term_count):
    real_table = []
    imag_table = []
    for term_order in range(term_count + 1):
        magnitude = (1.0 if term_order == 0 else 2.0) * bessel_first(term_order, evolve_time)
        quarter = term_order % 4
        real_table.append(magnitude if quarter == 0 else -magnitude if quarter == 2 else 0.0)
        imag_table.append(-magnitude if quarter == 1 else magnitude if quarter == 3 else 0.0)
    return (real_table, imag_table)


def spin_strengths(config_index, coupling_first, coupling_second, frozen_coupling, frozen_bits):
    spin_bits = config_index[:, None] >> jnp.arange(SPINS, dtype=jnp.int32)[None, :] & 1
    spin_signs = (1 - 2 * spin_bits).astype(jnp.float32)
    frozen_signs = (1 - 2 * frozen_bits).astype(jnp.float32)
    frozen_part = jnp.sum(frozen_coupling * frozen_signs)
    total_first = jnp.sum(coupling_first) + jnp.sum(frozen_coupling)
    strength_first = (
        ladder_first
        * (jnp.sum(spin_signs * coupling_first[None, :], axis=1) + frozen_part)
        / total_first
    )
    strength_second = (
        ladder_second
        * jnp.sum(spin_signs * coupling_second[None, :], axis=1)
        / jnp.sum(coupling_second)
    )
    return (strength_first, strength_second)


def apply_hamiltonian(padded, first_level, strength_first, strength_second, cutoff_rows):
    column_count = padded.shape[2] - 2 * FB
    center = padded[:, :, FB : FB + column_count]
    lower_level = padded[:, :, :column_count]
    upper_level = padded[:, :, 2 * FB :]
    column = lax.broadcasted_iota(jnp.int32, (1, column_count), 1)
    level_index = first_level + column // FB
    sub_index = column % FB
    cutoff = cutoff_rows[:, None]
    level_float = level_index.astype(jnp.float32)
    sub_float = sub_index.astype(jnp.float32)
    mode_low = jnp.where(
        (level_index >= 1) & (level_index < cutoff),
        jnp.sqrt(jnp.maximum(level_float, 0.0) / FA),
        0.0,
    )
    mode_high = jnp.where(
        (level_index + 1 >= 1) & (level_index + 1 < cutoff),
        jnp.sqrt(jnp.maximum(level_float + 1.0, 0.0) / FA),
        0.0,
    )
    sub_low = jnp.sqrt(sub_float / FB)
    sub_high = jnp.where(sub_index + 1 < FB, jnp.sqrt((sub_float + 1.0) / FB), 0.0)
    diagonal = diagonal_first * (2.0 * level_float / (FA - 1) - 1.0) + diagonal_second * (
        2.0 * sub_float / (FB - 1) - 1.0
    )
    previous_sub = jnp.pad(center[:, :, :-1], ((0, 0), (0, 0), (1, 0)))
    next_sub = jnp.pad(center[:, :, 1:], ((0, 0), (0, 0), (0, 1)))
    first_term = strength_first[None, :, None] * (
        mode_low[None] * lower_level + mode_high[None] * upper_level
    )
    second_term = strength_second[None, :, None] * (
        sub_low[None] * previous_sub + sub_high[None] * next_sub
    )
    return diagonal[None] * center + first_term + second_term


def weighted_term(term_vector, real_weight, imag_weight):
    rotated = jnp.stack([-term_vector[1], term_vector[0]])
    return real_weight * term_vector + imag_weight * rotated


def chebyshev_series(vector, apply_operator, term_count):
    real_table, imag_table = coefficient_table(term_count)
    real_weights = jnp.asarray(real_table, dtype=jnp.float32)
    imag_weights = jnp.asarray(imag_table, dtype=jnp.float32)
    current = apply_operator(vector)
    running = weighted_term(vector, real_weights[0], imag_weights[0]) + weighted_term(
        current, real_weights[1], imag_weights[1]
    )

    def advance(term_index, loop_state):
        previous, present, total = loop_state
        following = 2.0 * apply_operator(present) - previous
        total = total + weighted_term(following, real_weights[term_index], imag_weights[term_index])
        return (present, following, total)

    loop_state = lax.fori_loop(2, term_count + 1, advance, (vector, current, running))
    return loop_state[2]


def partner_term(own_part, partner, cosine, sine_value, phase_bit, side_sign):
    keep_part = 1.0 - phase_bit
    real_part = cosine * own_part[0] + sine_value * (
        side_sign * phase_bit * partner[0] + keep_part * partner[1]
    )
    imag_part = cosine * own_part[1] + sine_value * (
        side_sign * phase_bit * partner[1] - keep_part * partner[0]
    )
    return jnp.stack([real_part, imag_part])


def rotate_bits(vector, bit_list, angles, drive_bits):
    cosines = jnp.cos(angles)
    sine_values = jnp.sin(angles)
    phases = drive_bits.astype(jnp.float32)
    for spin_slot, bit_number in bit_list:
        config_total = vector.shape[1]
        lower_size = 1 << bit_number
        shaped = vector.reshape(2, config_total // (2 * lower_size), 2, lower_size, vector.shape[2])
        lower_half = shaped[:, :, 0]
        upper_half = shaped[:, :, 1]
        new_lower = partner_term(
            lower_half,
            upper_half,
            cosines[spin_slot],
            sine_values[spin_slot],
            phases[spin_slot],
            -1.0,
        )
        new_upper = partner_term(
            upper_half,
            lower_half,
            cosines[spin_slot],
            sine_values[spin_slot],
            phases[spin_slot],
            1.0,
        )
        vector = jnp.stack([new_lower, new_upper], axis=2).reshape(vector.shape)
    return vector


def per_device(
    amplitudes,
    cutoffs,
    coupling_first,
    coupling_second,
    frozen_coupling,
    frozen_bits,
    drive_bits,
    angles,
):
    local_configs = amplitudes.shape[1]
    column_count = amplitudes.shape[2]
    levels_here = column_count // FB
    spin_place = lax.axis_index("spin")
    fock_place = lax.axis_index("fock")
    config_index = spin_place * local_configs + lax.iota(jnp.int32, local_configs)
    strength_first, strength_second = spin_strengths(
        config_index, coupling_first, coupling_second, frozen_coupling, frozen_bits
    )
    first_level = fock_place * levels_here

    def apply_operator(field):
        padded = extended(field, (("fock", 2),), FB)
        return apply_hamiltonian(padded, first_level, strength_first, strength_second, cutoffs)

    propagated = chebyshev_series(amplitudes, apply_operator, DEGREE)
    local_bits = local_configs.bit_length() - 1
    spin_count = lax.axis_size("spin")
    split_bits = spin_count.bit_length() - 1
    result = rotate_bits(
        propagated, [(slot, slot) for slot in range(local_bits)], angles, drive_bits
    )
    rest = local_configs // spin_count
    rest_bits = rest.bit_length() - 1
    grouped = result.reshape(2, 1, spin_count, rest, column_count)
    moved = lax.all_to_all(grouped, "spin", split_axis=2, concat_axis=1, tiled=True)
    moved = rotate_bits(
        moved.reshape(2, spin_count * rest, column_count),
        [(local_bits + bit_number, rest_bits + bit_number) for bit_number in range(split_bits)],
        angles,
        drive_bits,
    )
    returned = lax.all_to_all(
        moved.reshape(2, spin_count, 1, rest, column_count),
        "spin",
        split_axis=1,
        concat_axis=2,
        tiled=True,
    )
    return returned.reshape(2, local_configs, column_count)


def solution(mesh):
    placed = (P(None, "spin", "fock"), P("spin"), P(), P(), P(), P(), P(), P())
    return jax.shard_map(
        per_device, mesh=mesh, in_specs=placed, out_specs=P(None, "spin", "fock"), check_vma=False
    )
```

profile of v0, /device:TPU:26, one launch (start us, length us, event | category | flops | bytes accessed | tf_op | source)
XLA Modules:
  0.0 3082.8 jit_solution(13448597303574678180)
XLA Ops:
  24.3 24.8 fusion.145
  85.1 39.8 %fusion.35 = f32[2,2048,1024]{1,2,0:T(8,128)} fusion(f32[2,2048,16]{1,2,0:T(8,128)S(1)} %collective-permute-done.3, f32[2,2048,1024]{1,2,0:T(8,128)} %copy.669, f32[2,2048,16]{1,2,0:T(8,128)S(1)} %collective-permute-done.2, f32[2,2048,1023]{1,2,0:T(8,128)} %get-tuple-element.532, f32[2,2048,1023]{1,2,0:T(8,128)} %get-tuple-element.531, ...), kind=kLoop, calls=%fused_computation.51 | loop fusion | flops 54525952 | bytes 84406272 | tf_op jit(solution)/shard_map/add | solution.py:107
  134.5 26.7 fusion.38
  161.2 1996.7 %while.22 = (s32[]{:T(128)}, f32[2,2048,1024]{1,2,0:T(8,128)}, f32[2,2048,1024]{1,2,0:T(8,128)}, f32[2,2048,1024]{1,2,0:T(8,128)}, s32[]{:T(128)}, /*index=5*/f3...) while((s32[]{:T(128)}, f32[2,2048,1024]{1,2,0:T(8,128)}, ...), condition=%wide.region_7.8_spmd.clone, body=%wide.region_6.7_spmd.sunk.clone.sunk | while | flops 98639872 | bytes 406442432 | solution.py:130
  167.3 22.2 fusion.159
  198.2 44.7 %fusion.163 = f32[2,2048,1024]{1,2,0:T(8,128)} fusion(f32[2,2048,1024]{1,2,0:T(8,128)} %get-tuple-element.688, f32[2,2048,16]{1,2,0:T(8,128)S(1)} %collective-permute-done, f32[2,2048,1024]{1,2,0:T(8,128)} %get-tuple-element.689, f32[2,2048,16]{1,2,0:T(8,128)S(1)} %collective-permute-done.1, f32[2,2048,1023]{1,2,0:T(8,128)} %get-tuple-element.659, ...), kind=kLoop, calls=%fused_computation.7.clone.1 | loop fusion | flops 62914560 | bytes 101183488 | tf_op jit(solution)/shard_map/while/body/eval_jaxpr/sub | solution.py:126
  274.3 18.4 fusion.164
  299.8 22.2 fusion.159
  330.7 44.7 %fusion.163 = f32[2,2048,1024]{1,2,0:T(8,128)} fusion(f32[2,2048,1024]{1,2,0:T(8,128)} %get-tuple-element.688, f32[2,2048,16]{1,2,0:T(8,128)S(1)} %collective-permute-done, f32[2,2048,1024]{1,2,0:T(8,128)} %get-tuple-element.689, f32[2,2048,16]{1,2,0:T(8,128)S(1)} %collective-permute-done.1, f32[2,2048,1023]{1,2,0:T(8,128)} %get-tuple-element.659, ...), kind=kLoop, calls=%fused_computation.7.clone.1 | loop fusion | flops 62914560 | bytes 101183488 | tf_op jit(solution)/shard_map/while/body/eval_jaxpr/sub | solution.py:126
  406.8 18.4 fusion.164
  432.3 22.2 fusion.159
  463.3 44.7 %fusion.163 = f32[2,2048,1024]{1,2,0:T(8,128)} fusion(f32[2,2048,1024]{1,2,0:T(8,128)} %get-tuple-element.688, f32[2,2048,16]{1,2,0:T(8,128)S(1)} %collective-permute-done, f32[2,2048,1024]{1,2,0:T(8,128)} %get-tuple-element.689, f32[2,2048,16]{1,2,0:T(8,128)S(1)} %collective-permute-done.1, f32[2,2048,1023]{1,2,0:T(8,128)} %get-tuple-element.659, ...), kind=kLoop, calls=%fused_computation.7.clone.1 | loop fusion | flops 62914560 | bytes 101183488 | tf_op jit(solution)/shard_map/while/body/eval_jaxpr/sub | solution.py:126
  539.3 18.4 fusion.164
  565.1 22.2 fusion.159
  596.0 44.7 %fusion.163 = f32[2,2048,1024]{1,2,0:T(8,128)} fusion(f32[2,2048,1024]{1,2,0:T(8,128)} %get-tuple-element.688, f32[2,2048,16]{1,2,0:T(8,128)S(1)} %collective-permute-done, f32[2,2048,1024]{1,2,0:T(8,128)} %get-tuple-element.689, f32[2,2048,16]{1,2,0:T(8,128)S(1)} %collective-permute-done.1, f32[2,2048,1023]{1,2,0:T(8,128)} %get-tuple-element.659, ...), kind=kLoop, calls=%fused_computation.7.clone.1 | loop fusion | flops 62914560 | bytes 101183488 | tf_op jit(solution)/shard_map/while/body/eval_jaxpr/sub | solution.py:126
  672.1 18.4 fusion.164
  698.5 22.2 fusion.159
  729.4 44.7 %fusion.163 = f32[2,2048,1024]{1,2,0:T(8,128)} fusion(f32[2,2048,1024]{1,2,0:T(8,128)} %get-tuple-element.688, f32[2,2048,16]{1,2,0:T(8,128)S(1)} %collective-permute-done, f32[2,2048,1024]{1,2,0:T(8,128)} %get-tuple-element.689, f32[2,2048,16]{1,2,0:T(8,128)S(1)} %collective-permute-done.1, f32[2,2048,1023]{1,2,0:T(8,128)} %get-tuple-element.659, ...), kind=kLoop, calls=%fused_computation.7.clone.1 | loop fusion | flops 62914560 | bytes 101183488 | tf_op jit(solution)/shard_map/while/body/eval_jaxpr/sub | solution.py:126
  831.9 22.2 fusion.159
  862.8 44.7 %fusion.163 = f32[2,2048,1024]{1,2,0:T(8,128)} fusion(f32[2,2048,1024]{1,2,0:T(8,128)} %get-tuple-element.688, f32[2,2048,16]{1,2,0:T(8,128)S(1)} %collective-permute-done, f32[2,2048,1024]{1,2,0:T(8,128)} %get-tuple-element.689, f32[2,2048,16]{1,2,0:T(8,128)S(1)} %collective-permute-done.1, f32[2,2048,1023]{1,2,0:T(8,128)} %get-tuple-element.659, ...), kind=kLoop, calls=%fused_computation.7.clone.1 | loop fusion | flops 62914560 | bytes 101183488 | tf_op jit(solution)/shard_map/while/body/eval_jaxpr/sub | solution.py:126
  938.9 18.4 fusion.164
  965.3 22.2 fusion.159
  996.2 44.7 %fusion.163 = f32[2,2048,1024]{1,2,0:T(8,128)} fusion(f32[2,2048,1024]{1,2,0:T(8,128)} %get-tuple-element.688, f32[2,2048,16]{1,2,0:T(8,128)S(1)} %collective-permute-done, f32[2,2048,1024]{1,2,0:T(8,128)} %get-tuple-element.689, f32[2,2048,16]{1,2,0:T(8,128)S(1)} %collective-permute-done.1, f32[2,2048,1023]{1,2,0:T(8,128)} %get-tuple-element.659, ...), kind=kLoop, calls=%fused_computation.7.clone.1 | loop fusion | flops 62914560 | bytes 101183488 | tf_op jit(solution)/shard_map/while/body/eval_jaxpr/sub | solution.py:126
  1072.3 18.4 fusion.164
  1098.7 22.2 fusion.159
  1129.6 44.7 %fusion.163 = f32[2,2048,1024]{1,2,0:T(8,128)} fusion(f32[2,2048,1024]{1,2,0:T(8,128)} %get-tuple-element.688, f32[2,2048,16]{1,2,0:T(8,128)S(1)} %collective-permute-done, f32[2,2048,1024]{1,2,0:T(8,128)} %get-tuple-element.689, f32[2,2048,16]{1,2,0:T(8,128)S(1)} %collective-permute-done.1, f32[2,2048,1023]{1,2,0:T(8,128)} %get-tuple-element.659, ...), kind=kLoop, calls=%fused_computation.7.clone.1 | loop fusion | flops 62914560 | bytes 101183488 | tf_op jit(solution)/shard_map/while/body/eval_jaxpr/sub | solution.py:126
  1232.1 22.2 fusion.159
  1263.0 44.7 %fusion.163 = f32[2,2048,1024]{1,2,0:T(8,128)} fusion(f32[2,2048,1024]{1,2,0:T(8,128)} %get-tuple-element.688, f32[2,2048,16]{1,2,0:T(8,128)S(1)} %collective-permute-done, f32[2,2048,1024]{1,2,0:T(8,128)} %get-tuple-element.689, f32[2,2048,16]{1,2,0:T(8,128)S(1)} %collective-permute-done.1, f32[2,2048,1023]{1,2,0:T(8,128)} %get-tuple-element.659, ...), kind=kLoop, calls=%fused_computation.7.clone.1 | loop fusion | flops 62914560 | bytes 101183488 | tf_op jit(solution)/shard_map/while/body/eval_jaxpr/sub | solution.py:126
  1339.1 18.4 fusion.164
  1365.5 22.2 fusion.159
  1396.4 44.7 %fusion.163 = f32[2,2048,1024]{1,2,0:T(8,128)} fusion(f32[2,2048,1024]{1,2,0:T(8,128)} %get-tuple-element.688, f32[2,2048,16]{1,2,0:T(8,128)S(1)} %collective-permute-done, f32[2,2048,1024]{1,2,0:T(8,128)} %get-tuple-element.689, f32[2,2048,16]{1,2,0:T(8,128)S(1)} %collective-permute-done.1, f32[2,2048,1023]{1,2,0:T(8,128)} %get-tuple-element.659, ...), kind=kLoop, calls=%fused_computation.7.clone.1 | loop fusion | flops 62914560 | bytes 101183488 | tf_op jit(solution)/shard_map/while/body/eval_jaxpr/sub | solution.py:126
  1472.5 18.4 fusion.164
  1498.9 22.2 fusion.159
  1529.8 44.7 %fusion.163 = f32[2,2048,1024]{1,2,0:T(8,128)} fusion(f32[2,2048,1024]{1,2,0:T(8,128)} %get-tuple-element.688, f32[2,2048,16]{1,2,0:T(8,128)S(1)} %collective-permute-done, f32[2,2048,1024]{1,2,0:T(8,128)} %get-tuple-element.689, f32[2,2048,16]{1,2,0:T(8,128)S(1)} %collective-permute-done.1, f32[2,2048,1023]{1,2,0:T(8,128)} %get-tuple-element.659, ...), kind=kLoop, calls=%fused_computation.7.clone.1 | loop fusion | flops 62914560 | bytes 101183488 | tf_op jit(solution)/shard_map/while/body/eval_jaxpr/sub | solution.py:126
  1632.3 22.2 fusion.159
  1663.2 44.7 %fusion.163 = f32[2,2048,1024]{1,2,0:T(8,128)} fusion(f32[2,2048,1024]{1,2,0:T(8,128)} %get-tuple-element.688, f32[2,2048,16]{1,2,0:T(8,128)S(1)} %collective-permute-done, f32[2,2048,1024]{1,2,0:T(8,128)} %get-tuple-element.689, f32[2,2048,16]{1,2,0:T(8,128)S(1)} %collective-permute-done.1, f32[2,2048,1023]{1,2,0:T(8,128)} %get-tuple-element.659, ...), kind=kLoop, calls=%fused_computation.7.clone.1 | loop fusion | flops 62914560 | bytes 101183488 | tf_op jit(solution)/shard_map/while/body/eval_jaxpr/sub | solution.py:126
  1765.7 22.2 fusion.159
  1796.6 44.7 %fusion.163 = f32[2,2048,1024]{1,2,0:T(8,128)} fusion(f32[2,2048,1024]{1,2,0:T(8,128)} %get-tuple-element.688, f32[2,2048,16]{1,2,0:T(8,128)S(1)} %collective-permute-done, f32[2,2048,1024]{1,2,0:T(8,128)} %get-tuple-element.689, f32[2,2048,16]{1,2,0:T(8,128)S(1)} %collective-permute-done.1, f32[2,2048,1023]{1,2,0:T(8,128)} %get-tuple-element.659, ...), kind=kLoop, calls=%fused_computation.7.clone.1 | loop fusion | flops 62914560 | bytes 101183488 | tf_op jit(solution)/shard_map/while/body/eval_jaxpr/sub | solution.py:126
  1899.1 22.2 fusion.159
  1930.0 44.7 %fusion.163 = f32[2,2048,1024]{1,2,0:T(8,128)} fusion(f32[2,2048,1024]{1,2,0:T(8,128)} %get-tuple-element.688, f32[2,2048,16]{1,2,0:T(8,128)S(1)} %collective-permute-done, f32[2,2048,1024]{1,2,0:T(8,128)} %get-tuple-element.689, f32[2,2048,16]{1,2,0:T(8,128)S(1)} %collective-permute-done.1, f32[2,2048,1023]{1,2,0:T(8,128)} %get-tuple-element.659, ...), kind=kLoop, calls=%fused_computation.7.clone.1 | loop fusion | flops 62914560 | bytes 101183488 | tf_op jit(solution)/shard_map/while/body/eval_jaxpr/sub | solution.py:126
  2032.5 22.2 fusion.159
  2063.4 44.7 %fusion.163 = f32[2,2048,1024]{1,2,0:T(8,128)} fusion(f32[2,2048,1024]{1,2,0:T(8,128)} %get-tuple-element.688, f32[2,2048,16]{1,2,0:T(8,128)S(1)} %collective-permute-done, f32[2,2048,1024]{1,2,0:T(8,128)} %get-tuple-element.689, f32[2,2048,16]{1,2,0:T(8,128)S(1)} %collective-permute-done.1, f32[2,2048,1023]{1,2,0:T(8,128)} %get-tuple-element.659, ...), kind=kLoop, calls=%fused_computation.7.clone.1 | loop fusion | flops 62914560 | bytes 101183488 | tf_op jit(solution)/shard_map/while/body/eval_jaxpr/sub | solution.py:126
  2157.9 25.3 copy.670
  2259.4 33.6 %add_bitcast_fusion.20 = (f32[1,512,2,1024]{3,0,2,1:T(1,128)}, f32[1,512,2,1024]{3,0,2,1:T(1,128)}, f32[1,512,2,1024]{3,0,2,1:T(1,128)S(1)}, f32[1,512,2,1024]{3,0,2,1:T(1,128)}) fusion(f32[]{:T(128)S(6)} %sub.409, f32[]{:T(128)S(6)} %mul.3378, f32[]{:T(128)} %bitcast.16, f32[]{:T(128)} %bitcast.11, f32[2,512,2,2,1024]{4,0,3,2,1:T(2,128)S(1)} %maximum_maximum_fusion, ...), kind=kLoop, calls=%fused_computation.256 | loop fusion | flops 25165824 | bytes 33554452 | tf_op jit(solution)/shard_map/add | solution.py:136
  2322.5 35.2 %add_bitcast_fusion.16 = (f32[1,256,4,1024]{3,0,2,1:T(1,128)}, f32[1,256,4,1024]{3,0,2,1:T(1,128)}, f32[1,256,4,1024]{3,0,2,1:T(1,128)S(1)}, f32[1,256,4,1024]{3,0,2,1:T(1,128)}) fusion(f32[]{:T(128)S(6)} %sub.412, f32[]{:T(128)S(6)} %mul.3399, f32[]{:T(128)} %bitcast.26, f32[]{:T(128)} %bitcast.10, f32[2,256,2,4,1024]{4,0,3,2,1:T(2,128)S(1)} %bitcast.692, ...), kind=kLoop, calls=%fused_computation.252 | loop fusion | flops 25165824 | bytes 33554452 | tf_op jit(solution)/shard_map/add | solution.py:136
  2392.1 35.0 %add_bitcast_fusion.12 = (f32[1,128,8,1024]{3,0,2,1:T(1,128)}, f32[1,128,8,1024]{3,0,2,1:T(1,128)}, f32[1,128,8,1024]{3,0,2,1:T(1,128)S(1)}, f32[1,128,8,1024]{3,0,2,1:T(1,128)}) fusion(f32[]{:T(128)S(6)} %sub.415, f32[]{:T(128)S(6)} %mul.3420, f32[]{:T(128)} %bitcast.35, f32[]{:T(128)} %bitcast.9, f32[2,128,2,8,1024]{4,0,3,2,1:T(2,128)S(1)} %bitcast.693, ...), kind=kLoop, calls=%fused_computation.248 | loop fusion | flops 25165824 | bytes 33554452 | tf_op jit(solution)/shard_map/add | solution.py:136
  2647.1 180.4 %all-to-all-done = f32[2,1,4,512,1024]{4,3,0,1,2:T(8,128)} async-done(((f32[2,1,4,512,1024]{4,3,0,1,2:T(8,128)}), f32[2,1,4,512,1024]{4,3,0,1,2:T(8,128)}, u32[]{:S(2)}, u32[]{:S(2)}) %all-to-all-start) | async-done | bytes 16777248 | tf_op jit(solution)/shard_map/all_to_all | solution.py:210
  2890.0 186.1 %all_to_all.8 = f32[2,4,1,512,1024]{4,3,0,2,1:T(8,128)S(1)} all-to-all(f32[2,4,1,512,1024]{4,3,0,2,1:T(8,128)S(1)} %copy.776), channel_id=1, replica_groups=mesh['spin'=4,'fock'=8] {'spin'}, dimensions={1} | all-to-all | bytes 33554432 | tf_op jit(solution)/shard_map/all_to_all | solution.py:217
  (632 shorter events, 1324.3 us)
Async XLA Ops:
  18.4 66.7 %collective-permute-start.2 = (f32[2,2048,16]{1,2,0:T(8,128)S(1)}, f32[2,2048,16]{1,2,0:T(8,128)S(1)}, u32[]{:S(2)}, u32[]{:S(2)}) collective-permute-start(f32[2,2048,16]{1,2,0:T(8,128)S(1)} %get-tuple-element.533), channel_id=1, source_target_pairs={{0,1},{1,2},{2,3},{3,4},{4,5},{5,6},{6,7},{8,9},{9,10},{10,11},{11... | collective-permute-start | bytes 786440 | tf_op jit(solution)/shard_map/ppermute | solution.py:28
  19.7 65.4 %collective-permute-start.3 = (f32[2,2048,16]{1,2,0:T(8,128)S(1)}, f32[2,2048,16]{1,2,0:T(8,128)S(1)}, u32[]{:S(2)}, u32[]{:S(2)}) collective-permute-start(f32[2,2048,16]{1,2,0:T(8,128)S(1)} %get-tuple-element.534), channel_id=1, source_target_pairs={{1,0},{2,1},{3,2},{4,3},{5,4},{6,5},{7,6},{9,8},{10,9},{11,10},{12... | collective-permute-start | bytes 786440 | tf_op jit(solution)/shard_map/ppermute | solution.py:29
  24.3 26.8 copy-start
  134.5 26.7 copy-start.9
  134.5 26.7 copy-start.16
  134.5 26.7 copy-start.17
  162.6 35.6 %collective-permute-start = (f32[2,2048,16]{1,2,0:T(8,128)S(1)}, f32[2,2048,16]{1,2,0:T(8,128)S(1)}, u32[]{:S(2)}, u32[]{:S(2)}) collective-permute-start(f32[2,2048,16]{1,2,0:T(8,128)S(1)} %get-tuple-element.657), channel_id=1, source_target_pairs={{1,0},{2,1},{3,2},{4,3},{5,4},{6,5},{7,6},{9,8},{10,9},{11,10},{12... | collective-permute-start | bytes 786440 | tf_op jit(solution)/shard_map/while/body/eval_jaxpr/ppermute | solution.py:29
  165.9 32.3 %collective-permute-start.1 = (f32[2,2048,16]{1,2,0:T(8,128)S(1)}, f32[2,2048,16]{1,2,0:T(8,128)S(1)}, u32[]{:S(2)}, u32[]{:S(2)}) collective-permute-start(f32[2,2048,16]{1,2,0:T(8,128)S(1)} %get-tuple-element.658), channel_id=1, source_target_pairs={{0,1},{1,2},{2,3},{3,4},{4,5},{5,6},{6,7},{8,9},{9,10},{10,11},{11... | collective-permute-start | bytes 786440 | tf_op jit(solution)/shard_map/while/body/eval_jaxpr/ppermute | solution.py:28
  242.9 25.6 slice-start
  293.9 36.8 %collective-permute-start = (f32[2,2048,16]{1,2,0:T(8,128)S(1)}, f32[2,2048,16]{1,2,0:T(8,128)S(1)}, u32[]{:S(2)}, u32[]{:S(2)}) collective-permute-start(f32[2,2048,16]{1,2,0:T(8,128)S(1)} %get-tuple-element.657), channel_id=1, source_target_pairs={{1,0},{2,1},{3,2},{4,3},{5,4},{6,5},{7,6},{9,8},{10,9},{11,10},{12... | collective-permute-start | bytes 786440 | tf_op jit(solution)/shard_map/while/body/eval_jaxpr/ppermute | solution.py:29
  298.4 32.3 %collective-permute-start.1 = (f32[2,2048,16]{1,2,0:T(8,128)S(1)}, f32[2,2048,16]{1,2,0:T(8,128)S(1)}, u32[]{:S(2)}, u32[]{:S(2)}) collective-permute-start(f32[2,2048,16]{1,2,0:T(8,128)S(1)} %get-tuple-element.658), channel_id=1, source_target_pairs={{0,1},{1,2},{2,3},{3,4},{4,5},{5,6},{6,7},{8,9},{9,10},{10,11},{11... | collective-permute-start | bytes 786440 | tf_op jit(solution)/shard_map/while/body/eval_jaxpr/ppermute | solution.py:28
  375.4 25.6 slice-start
  426.4 36.8 %collective-permute-start = (f32[2,2048,16]{1,2,0:T(8,128)S(1)}, f32[2,2048,16]{1,2,0:T(8,128)S(1)}, u32[]{:S(2)}, u32[]{:S(2)}) collective-permute-start(f32[2,2048,16]{1,2,0:T(8,128)S(1)} %get-tuple-element.657), channel_id=1, source_target_pairs={{1,0},{2,1},{3,2},{4,3},{5,4},{6,5},{7,6},{9,8},{10,9},{11,10},{12... | collective-permute-start | bytes 786440 | tf_op jit(solution)/shard_map/while/body/eval_jaxpr/ppermute | solution.py:29
  431.0 32.3 %collective-permute-start.1 = (f32[2,2048,16]{1,2,0:T(8,128)S(1)}, f32[2,2048,16]{1,2,0:T(8,128)S(1)}, u32[]{:S(2)}, u32[]{:S(2)}) collective-permute-start(f32[2,2048,16]{1,2,0:T(8,128)S(1)} %get-tuple-element.658), channel_id=1, source_target_pairs={{0,1},{1,2},{2,3},{3,4},{4,5},{5,6},{6,7},{8,9},{9,10},{10,11},{11... | collective-permute-start | bytes 786440 | tf_op jit(solution)/shard_map/while/body/eval_jaxpr/ppermute | solution.py:28
  507.9 25.6 slice-start
  558.9 37.1 %collective-permute-start = (f32[2,2048,16]{1,2,0:T(8,128)S(1)}, f32[2,2048,16]{1,2,0:T(8,128)S(1)}, u32[]{:S(2)}, u32[]{:S(2)}) collective-permute-start(f32[2,2048,16]{1,2,0:T(8,128)S(1)} %get-tuple-element.657), channel_id=1, source_target_pairs={{1,0},{2,1},{3,2},{4,3},{5,4},{6,5},{7,6},{9,8},{10,9},{11,10},{12... | collective-permute-start | bytes 786440 | tf_op jit(solution)/shard_map/while/body/eval_jaxpr/ppermute | solution.py:29
  563.7 32.3 %collective-permute-start.1 = (f32[2,2048,16]{1,2,0:T(8,128)S(1)}, f32[2,2048,16]{1,2,0:T(8,128)S(1)}, u32[]{:S(2)}, u32[]{:S(2)}) collective-permute-start(f32[2,2048,16]{1,2,0:T(8,128)S(1)} %get-tuple-element.658), channel_id=1, source_target_pairs={{0,1},{1,2},{2,3},{3,4},{4,5},{5,6},{6,7},{8,9},{9,10},{10,11},{11... | collective-permute-start | bytes 786440 | tf_op jit(solution)/shard_map/while/body/eval_jaxpr/ppermute | solution.py:28
  640.7 25.6 slice-start
  691.6 37.7 %collective-permute-start = (f32[2,2048,16]{1,2,0:T(8,128)S(1)}, f32[2,2048,16]{1,2,0:T(8,128)S(1)}, u32[]{:S(2)}, u32[]{:S(2)}) collective-permute-start(f32[2,2048,16]{1,2,0:T(8,128)S(1)} %get-tuple-element.657), channel_id=1, source_target_pairs={{1,0},{2,1},{3,2},{4,3},{5,4},{6,5},{7,6},{9,8},{10,9},{11,10},{12... | collective-permute-start | bytes 786440 | tf_op jit(solution)/shard_map/while/body/eval_jaxpr/ppermute | solution.py:29
  697.1 32.3 %collective-permute-start.1 = (f32[2,2048,16]{1,2,0:T(8,128)S(1)}, f32[2,2048,16]{1,2,0:T(8,128)S(1)}, u32[]{:S(2)}, u32[]{:S(2)}) collective-permute-start(f32[2,2048,16]{1,2,0:T(8,128)S(1)} %get-tuple-element.658), channel_id=1, source_target_pairs={{0,1},{1,2},{2,3},{3,4},{4,5},{5,6},{6,7},{8,9},{9,10},{10,11},{11... | collective-permute-start | bytes 786440 | tf_op jit(solution)/shard_map/while/body/eval_jaxpr/ppermute | solution.py:28
  774.1 25.6 slice-start
  825.0 37.7 %collective-permute-start = (f32[2,2048,16]{1,2,0:T(8,128)S(1)}, f32[2,2048,16]{1,2,0:T(8,128)S(1)}, u32[]{:S(2)}, u32[]{:S(2)}) collective-permute-start(f32[2,2048,16]{1,2,0:T(8,128)S(1)} %get-tuple-element.657), channel_id=1, source_target_pairs={{1,0},{2,1},{3,2},{4,3},{5,4},{6,5},{7,6},{9,8},{10,9},{11,10},{12... | collective-permute-start | bytes 786440 | tf_op jit(solution)/shard_map/while/body/eval_jaxpr/ppermute | solution.py:29
  830.5 32.3 %collective-permute-start.1 = (f32[2,2048,16]{1,2,0:T(8,128)S(1)}, f32[2,2048,16]{1,2,0:T(8,128)S(1)}, u32[]{:S(2)}, u32[]{:S(2)}) collective-permute-start(f32[2,2048,16]{1,2,0:T(8,128)S(1)} %get-tuple-element.658), channel_id=1, source_target_pairs={{0,1},{1,2},{2,3},{3,4},{4,5},{5,6},{6,7},{8,9},{9,10},{10,11},{11... | collective-permute-start | bytes 786440 | tf_op jit(solution)/shard_map/while/body/eval_jaxpr/ppermute | solution.py:28
  907.5 25.6 slice-start
  958.4 37.7 %collective-permute-start = (f32[2,2048,16]{1,2,0:T(8,128)S(1)}, f32[2,2048,16]{1,2,0:T(8,128)S(1)}, u32[]{:S(2)}, u32[]{:S(2)}) collective-permute-start(f32[2,2048,16]{1,2,0:T(8,128)S(1)} %get-tuple-element.657), channel_id=1, source_target_pairs={{1,0},{2,1},{3,2},{4,3},{5,4},{6,5},{7,6},{9,8},{10,9},{11,10},{12... | collective-permute-start | bytes 786440 | tf_op jit(solution)/shard_map/while/body/eval_jaxpr/ppermute | solution.py:29
  963.9 32.3 %collective-permute-start.1 = (f32[2,2048,16]{1,2,0:T(8,128)S(1)}, f32[2,2048,16]{1,2,0:T(8,128)S(1)}, u32[]{:S(2)}, u32[]{:S(2)}) collective-permute-start(f32[2,2048,16]{1,2,0:T(8,128)S(1)} %get-tuple-element.658), channel_id=1, source_target_pairs={{0,1},{1,2},{2,3},{3,4},{4,5},{5,6},{6,7},{8,9},{9,10},{10,11},{11... | collective-permute-start | bytes 786440 | tf_op jit(solution)/shard_map/while/body/eval_jaxpr/ppermute | solution.py:28
  1040.9 25.6 slice-start
  1091.8 37.7 %collective-permute-start = (f32[2,2048,16]{1,2,0:T(8,128)S(1)}, f32[2,2048,16]{1,2,0:T(8,128)S(1)}, u32[]{:S(2)}, u32[]{:S(2)}) collective-permute-start(f32[2,2048,16]{1,2,0:T(8,128)S(1)} %get-tuple-element.657), channel_id=1, source_target_pairs={{1,0},{2,1},{3,2},{4,3},{5,4},{6,5},{7,6},{9,8},{10,9},{11,10},{12... | collective-permute-start | bytes 786440 | tf_op jit(solution)/shard_map/while/body/eval_jaxpr/ppermute | solution.py:29
  1097.3 32.3 %collective-permute-start.1 = (f32[2,2048,16]{1,2,0:T(8,128)S(1)}, f32[2,2048,16]{1,2,0:T(8,128)S(1)}, u32[]{:S(2)}, u32[]{:S(2)}) collective-permute-start(f32[2,2048,16]{1,2,0:T(8,128)S(1)} %get-tuple-element.658), channel_id=1, source_target_pairs={{0,1},{1,2},{2,3},{3,4},{4,5},{5,6},{6,7},{8,9},{9,10},{10,11},{11... | collective-permute-start | bytes 786440 | tf_op jit(solution)/shard_map/while/body/eval_jaxpr/ppermute | solution.py:28
  1174.3 25.6 slice-start
  1225.2 37.7 %collective-permute-start = (f32[2,2048,16]{1,2,0:T(8,128)S(1)}, f32[2,2048,16]{1,2,0:T(8,128)S(1)}, u32[]{:S(2)}, u32[]{:S(2)}) collective-permute-start(f32[2,2048,16]{1,2,0:T(8,128)S(1)} %get-tuple-element.657), channel_id=1, source_target_pairs={{1,0},{2,1},{3,2},{4,3},{5,4},{6,5},{7,6},{9,8},{10,9},{11,10},{12... | collective-permute-start | bytes 786440 | tf_op jit(solution)/shard_map/while/body/eval_jaxpr/ppermute | solution.py:29
  1230.7 32.3 %collective-permute-start.1 = (f32[2,2048,16]{1,2,0:T(8,128)S(1)}, f32[2,2048,16]{1,2,0:T(8,128)S(1)}, u32[]{:S(2)}, u32[]{:S(2)}) collective-permute-start(f32[2,2048,16]{1,2,0:T(8,128)S(1)} %get-tuple-element.658), channel_id=1, source_target_pairs={{0,1},{1,2},{2,3},{3,4},{4,5},{5,6},{6,7},{8,9},{9,10},{10,11},{11... | collective-permute-start | bytes 786440 | tf_op jit(solution)/shard_map/while/body/eval_jaxpr/ppermute | solution.py:28
  1307.7 25.6 slice-start
  1358.6 37.7 %collective-permute-start = (f32[2,2048,16]{1,2,0:T(8,128)S(1)}, f32[2,2048,16]{1,2,0:T(8,128)S(1)}, u32[]{:S(2)}, u32[]{:S(2)}) collective-permute-start(f32[2,2048,16]{1,2,0:T(8,128)S(1)} %get-tuple-element.657), channel_id=1, source_target_pairs={{1,0},{2,1},{3,2},{4,3},{5,4},{6,5},{7,6},{9,8},{10,9},{11,10},{12... | collective-permute-start | bytes 786440 | tf_op jit(solution)/shard_map/while/body/eval_jaxpr/ppermute | solution.py:29
  1364.1 32.3 %collective-permute-start.1 = (f32[2,2048,16]{1,2,0:T(8,128)S(1)}, f32[2,2048,16]{1,2,0:T(8,128)S(1)}, u32[]{:S(2)}, u32[]{:S(2)}) collective-permute-start(f32[2,2048,16]{1,2,0:T(8,128)S(1)} %get-tuple-element.658), channel_id=1, source_target_pairs={{0,1},{1,2},{2,3},{3,4},{4,5},{5,6},{6,7},{8,9},{9,10},{10,11},{11... | collective-permute-start | bytes 786440 | tf_op jit(solution)/shard_map/while/body/eval_jaxpr/ppermute | solution.py:28
  1441.1 25.6 slice-start
  1492.0 37.7 %collective-permute-start = (f32[2,2048,16]{1,2,0:T(8,128)S(1)}, f32[2,2048,16]{1,2,0:T(8,128)S(1)}, u32[]{:S(2)}, u32[]{:S(2)}) collective-permute-start(f32[2,2048,16]{1,2,0:T(8,128)S(1)} %get-tuple-element.657), channel_id=1, source_target_pairs={{1,0},{2,1},{3,2},{4,3},{5,4},{6,5},{7,6},{9,8},{10,9},{11,10},{12... | collective-permute-start | bytes 786440 | tf_op jit(solution)/shard_map/while/body/eval_jaxpr/ppermute | solution.py:29
  1497.5 32.3 %collective-permute-start.1 = (f32[2,2048,16]{1,2,0:T(8,128)S(1)}, f32[2,2048,16]{1,2,0:T(8,128)S(1)}, u32[]{:S(2)}, u32[]{:S(2)}) collective-permute-start(f32[2,2048,16]{1,2,0:T(8,128)S(1)} %get-tuple-element.658), channel_id=1, source_target_pairs={{0,1},{1,2},{2,3},{3,4},{4,5},{5,6},{6,7},{8,9},{9,10},{10,11},{11... | collective-permute-start | bytes 786440 | tf_op jit(solution)/shard_map/while/body/eval_jaxpr/ppermute | solution.py:28
  1625.5 37.7 %collective-permute-start = (f32[2,2048,16]{1,2,0:T(8,128)S(1)}, f32[2,2048,16]{1,2,0:T(8,128)S(1)}, u32[]{:S(2)}, u32[]{:S(2)}) collective-permute-start(f32[2,2048,16]{1,2,0:T(8,128)S(1)} %get-tuple-element.657), channel_id=1, source_target_pairs={{1,0},{2,1},{3,2},{4,3},{5,4},{6,5},{7,6},{9,8},{10,9},{11,10},{12... | collective-permute-start | bytes 786440 | tf_op jit(solution)/shard_map/while/body/eval_jaxpr/ppermute | solution.py:29
  1630.9 32.3 %collective-permute-start.1 = (f32[2,2048,16]{1,2,0:T(8,128)S(1)}, f32[2,2048,16]{1,2,0:T(8,128)S(1)}, u32[]{:S(2)}, u32[]{:S(2)}) collective-permute-start(f32[2,2048,16]{1,2,0:T(8,128)S(1)} %get-tuple-element.658), channel_id=1, source_target_pairs={{0,1},{1,2},{2,3},{3,4},{4,5},{5,6},{6,7},{8,9},{9,10},{10,11},{11... | collective-permute-start | bytes 786440 | tf_op jit(solution)/shard_map/while/body/eval_jaxpr/ppermute | solution.py:28
  1758.9 37.7 %collective-permute-start = (f32[2,2048,16]{1,2,0:T(8,128)S(1)}, f32[2,2048,16]{1,2,0:T(8,128)S(1)}, u32[]{:S(2)}, u32[]{:S(2)}) collective-permute-start(f32[2,2048,16]{1,2,0:T(8,128)S(1)} %get-tuple-element.657), channel_id=1, source_target_pairs={{1,0},{2,1},{3,2},{4,3},{5,4},{6,5},{7,6},{9,8},{10,9},{11,10},{12... | collective-permute-start | bytes 786440 | tf_op jit(solution)/shard_map/while/body/eval_jaxpr/ppermute | solution.py:29
  1764.3 32.3 %collective-permute-start.1 = (f32[2,2048,16]{1,2,0:T(8,128)S(1)}, f32[2,2048,16]{1,2,0:T(8,128)S(1)}, u32[]{:S(2)}, u32[]{:S(2)}) collective-permute-start(f32[2,2048,16]{1,2,0:T(8,128)S(1)} %get-tuple-element.658), channel_id=1, source_target_pairs={{0,1},{1,2},{2,3},{3,4},{4,5},{5,6},{6,7},{8,9},{9,10},{10,11},{11... | collective-permute-start | bytes 786440 | tf_op jit(solution)/shard_map/while/body/eval_jaxpr/ppermute | solution.py:28
  1841.3 25.6 slice-start
  1892.3 37.7 %collective-permute-start = (f32[2,2048,16]{1,2,0:T(8,128)S(1)}, f32[2,2048,16]{1,2,0:T(8,128)S(1)}, u32[]{:S(2)}, u32[]{:S(2)}) collective-permute-start(f32[2,2048,16]{1,2,0:T(8,128)S(1)} %get-tuple-element.657), channel_id=1, source_target_pairs={{1,0},{2,1},{3,2},{4,3},{5,4},{6,5},{7,6},{9,8},{10,9},{11,10},{12... | collective-permute-start | bytes 786440 | tf_op jit(solution)/shard_map/while/body/eval_jaxpr/ppermute | solution.py:29
  1897.7 32.3 %collective-permute-start.1 = (f32[2,2048,16]{1,2,0:T(8,128)S(1)}, f32[2,2048,16]{1,2,0:T(8,128)S(1)}, u32[]{:S(2)}, u32[]{:S(2)}) collective-permute-start(f32[2,2048,16]{1,2,0:T(8,128)S(1)} %get-tuple-element.658), channel_id=1, source_target_pairs={{0,1},{1,2},{2,3},{3,4},{4,5},{5,6},{6,7},{8,9},{9,10},{10,11},{11... | collective-permute-start | bytes 786440 | tf_op jit(solution)/shard_map/while/body/eval_jaxpr/ppermute | solution.py:28
  2025.7 37.7 %collective-permute-start = (f32[2,2048,16]{1,2,0:T(8,128)S(1)}, f32[2,2048,16]{1,2,0:T(8,128)S(1)}, u32[]{:S(2)}, u32[]{:S(2)}) collective-permute-start(f32[2,2048,16]{1,2,0:T(8,128)S(1)} %get-tuple-element.657), channel_id=1, source_target_pairs={{1,0},{2,1},{3,2},{4,3},{5,4},{6,5},{7,6},{9,8},{10,9},{11,10},{12... | collective-permute-start | bytes 786440 | tf_op jit(solution)/shard_map/while/body/eval_jaxpr/ppermute | solution.py:29
  2031.1 32.3 %collective-permute-start.1 = (f32[2,2048,16]{1,2,0:T(8,128)S(1)}, f32[2,2048,16]{1,2,0:T(8,128)S(1)}, u32[]{:S(2)}, u32[]{:S(2)}) collective-permute-start(f32[2,2048,16]{1,2,0:T(8,128)S(1)} %get-tuple-element.658), channel_id=1, source_target_pairs={{0,1},{1,2},{2,3},{3,4},{4,5},{5,6},{6,7},{8,9},{9,10},{10,11},{11... | collective-permute-start | bytes 786440 | tf_op jit(solution)/shard_map/while/body/eval_jaxpr/ppermute | solution.py:28
  2637.2 190.3 %all-to-all-start = ((f32[2,1,4,512,1024]{4,3,0,1,2:T(8,128)}), f32[2,1,4,512,1024]{4,3,0,1,2:T(8,128)}, u32[]{:S(2)}, u32[]{:S(2)}) async-start(f32[2,1,4,512,1024]{4,3,0,1,2:T(8,128)} %copy.753), calls=%async_computation | async-start | bytes 33554432 | tf_op jit(solution)/shard_map/all_to_all | solution.py:210
  (119 other events, 1552.1 us)
where the time goes:
time: 3100 us; the launch traced here: 3080 us
  other arithmetic  1760 us (57%)
  local copies, waits for them, and re-layouts  828 us (27%)
  blocking collectives  186 us (6%)
  waiting for transfers between devices  180 us (6%)
  starting transfers between devices  110 us (4%)
    sub x15, other arithmetic, advance(): following = 2.0 * apply_operator(present) - previous  670 us
    slice x16, local copies, waits for them, and re-layouts, apply_hamiltonian(): previous_sub = jnp.pad(center[:, :, :-1], ((0, 0), (0, 0), (1, 0)))  358 us
    while x270, local copies, waits for them, and re-layouts  282 us
    add x15, other arithmetic, advance(): total + weighted_term(following, real_weights[term_index], imag_weights[t...  277 us
    neg x17, other arithmetic, weighted_term(): rotated = jnp.stack([-term_vector[1], term_vector[0]])  205 us
    another operation x37, other arithmetic, rotate_bits(): vector = jnp.stack([new_lower, new_upper], axis=2).reshape(vector.shape)  191 us
    all_to_all x1, blocking collectives, per_device(): lax.all_to_all(moved.reshape(2, spin_count, 1, rest, column_count), 'spin...  186 us
    all_to_all x1, waiting for transfers between devices, per_device(): lax.all_to_all(grouped, 'spin', split_axis=2, concat_axis=1, tiled=True)  180 us
  transfers between devices with their start and end apart: 33, of which 1 were waited for; matrix products, arithmetic and copies ran while one was open for 17% of the time, Pallas kernels for 0%

commit v1 on v0

v1 whole, which is shorter than its diff:
```python
import functools
import math

import jax
import jax.numpy as jnp
from jax import lax
from jax.experimental import pallas as pl
from jax.experimental.pallas import tpu as pltpu
from jax.sharding import PartitionSpec as P

SPINS = 13
FA = 512
FB = 16
DEGREE = 16

evolve_time = 12.0
diagonal_first = 0.06
diagonal_second = 0.04
ladder_first = 0.35
ladder_second = 0.1

LANES = 128
ROWS = 8
HALF = ROWS // 2
CUTS = 2
PARTS = 2 * CUTS
GROUP = 128
LOW_BITS = 7
VMEM_LIMIT = 48 * 1024 * 1024
NO_COST = pl.CostEstimate(flops=1, bytes_accessed=1, transcendentals=0)


def bessel_first(term_order, argument):
    running = 0.0
    addend = (argument / 2.0) ** term_order / math.factorial(term_order)
    for serial in range(80):
        running = running + addend
        addend = addend * -(argument * argument / 4.0) / ((serial + 1) * (serial + 1 + term_order))
    return running


def series_weights(term_count):
    weights = []
    for order in range(term_count + 1):
        magnitude = (1.0 if order == 0 else 2.0) * bessel_first(order, evolve_time)
        weights.append(magnitude if order % 4 in (0, 3) else -magnitude)
    return weights


def low_matrix(cosines, sines):
    out = lax.broadcasted_iota(jnp.int32, (GROUP, GROUP), 0)
    into = lax.broadcasted_iota(jnp.int32, (GROUP, GROUP), 1)
    result = jnp.ones((GROUP, GROUP), jnp.float32)
    for spin in range(LOW_BITS):
        out_bit, in_bit = (out >> spin) & 1, (into >> spin) & 1
        crossing = jnp.where(out_bit == 1, sines[spin], -sines[spin])
        result = result * jnp.where(out_bit == in_bit, cosines[spin], crossing)
    return result


def phase_of(config, drive_ref):
    quarter = jnp.zeros(config.shape, jnp.int32)
    for spin in range(SPINS):
        quarter = quarter + ((config >> spin) & 1) * (1 - drive_ref[spin])
    quarter = quarter & 3
    real = jnp.where(quarter == 0, 1.0, jnp.where(quarter == 2, -1.0, 0.0))
    imag = jnp.where(quarter == 1, 1.0, jnp.where(quarter == 3, -1.0, 0.0))
    return real, imag


def scalar_sum(ref):
    total = ref[0]
    for index in range(1, ref.shape[0]):
        total = total + ref[index]
    return total


SCALARS = pl.BlockSpec(memory_space=pltpu.SMEM)


def tied(value, *earlier):
    return lax.optimization_barrier((value, *earlier))[0]


def prepare_kernel(drive_ref, cosines, sines, matrix_ref, phases_ref):
    count = phases_ref.shape[0]
    matrix_ref[...] = low_matrix(cosines, sines)
    first_config = lax.axis_index("spin") * count
    column = lax.broadcasted_iota(jnp.int32, (GROUP, 8), 1)

    def fill(group, carry):
        config = first_config + group * GROUP + lax.broadcasted_iota(jnp.int32, (GROUP, 8), 0)
        real, imag = phase_of(config, drive_ref)
        rows = pl.ds(pl.multiple_of(group * GROUP, GROUP), GROUP)
        phases_ref[rows, :] = jnp.where(column == 0, real, imag)
        return carry

    lax.fori_loop(0, count // GROUP, fill, 0)


def prepare(drive_bits, cosines, sines, count):
    return pl.pallas_call(
        prepare_kernel,
        in_specs=[SCALARS] * 3,
        out_shape=[
            jax.ShapeDtypeStruct((GROUP, GROUP), jnp.float32),
            jax.ShapeDtypeStruct((count, 8), jnp.float32),
        ],
        cost_estimate=NO_COST,
        name="prepare",
    )(drive_bits, cosines, sines)


def series_kernel(
    weights,
    halves,
    flip,
    first_unit,
    first_coupling_ref,
    second_coupling_ref,
    frozen_coupling_ref,
    frozen_bits_ref,
    drive_ref,
    cutoff_ref,
    left_ref,
    middle_ref,
    right_ref,
    *refs,
):
    out_refs = refs[:PARTS]
    source, swapped, even_buffer, odd_buffer, ladder, diagonal = refs[PARTS:]
    halo_tiles = left_ref.shape[3] // LANES
    own_tiles = middle_ref.shape[3] // LANES
    tiles = halo_tiles + own_tiles + halo_tiles
    levels_per_tile = LANES // FB
    levels = tiles * levels_per_tile
    mirrored = halves == 2
    segments = HALF // halves
    depth = levels // segments
    block = FB * ROWS
    row = lax.broadcasted_iota(jnp.int32, (ROWS, LANES), 0)
    side = jnp.where(row < HALF, -1.0, 1.0)
    segment_row = row % segments
    first_level = lax.axis_index("fock") * (own_tiles * levels_per_tile) - DEGREE

    def level_at(index):
        if mirrored:
            return first_level + jnp.where(segment_row == 0, index, levels - 1 - index)
        return first_level + segment_row * depth + index

    def link_at(index):
        if mirrored:
            return first_level + jnp.where(segment_row == 0, index, levels - index)
        return level_at(index)

    def place_of(level):
        segment, index = divmod(level, depth)
        return segment, depth - 1 - index if mirrored and segment == 1 else index

    def register(index, sub):
        return pl.ds(pl.multiple_of(index * block + sub * ROWS, ROWS), ROWS)

    @pl.when(pl.program_id(0) == 0)
    def _():
        def fill(index, carry):
            level = level_at(index).astype(jnp.float32)
            first = diagonal_first * (2.0 * level / (FA - 1) - 1.0)
            for sub in range(FB):
                second = diagonal_second * (2.0 * sub / (FB - 1) - 1.0)
                diagonal[register(index, sub), :] = 2.0 * (first + second)
            return carry

        lax.fori_loop(0, depth, fill, 0)

    units_here = (1 << SPINS) // (GROUP * halves) // lax.axis_size("spin")
    unit = (lax.axis_index("spin") ^ flip) * units_here + first_unit + pl.program_id(0)
    half_row = (row % HALF) // segments
    lane = lax.broadcasted_iota(jnp.int32, (ROWS, LANES), 1)
    config = (unit * halves + half_row) * GROUP + lane
    sum_first = jnp.zeros((ROWS, LANES), jnp.float32)
    sum_second = jnp.zeros((ROWS, LANES), jnp.float32)
    for spin in range(SPINS):
        sign = (1 - 2 * ((config >> spin) & 1)).astype(jnp.float32)
        sum_first = sum_first + sign * first_coupling_ref[spin]
        sum_second = sum_second + sign * second_coupling_ref[spin]
    frozen_part = 0.0
    for index in range(frozen_bits_ref.shape[0]):
        frozen_sign = (1 - 2 * frozen_bits_ref[index]).astype(jnp.float32)
        frozen_part = frozen_part + frozen_coupling_ref[index] * frozen_sign
    total_first = scalar_sum(first_coupling_ref) + scalar_sum(frozen_coupling_ref)
    total_second = scalar_sum(second_coupling_ref)
    first = (2.0 * ladder_first) * (sum_first + frozen_part) / total_first
    second = (2.0 * ladder_second) * sum_second / total_second
    cutoff = jnp.broadcast_to(cutoff_ref[:, :LANES], (ROWS, LANES))
    if halves == 2:
        upper_cutoff = jnp.broadcast_to(cutoff_ref[:, LANES:], (ROWS, LANES))
        cutoff = jnp.where(half_row == 0, cutoff, upper_cutoff)
    cutoff = cutoff.astype(jnp.float32)
    phase_real, phase_imag = phase_of(config, drive_ref)
    for index in range(depth + 1):
        level_index = link_at(index)
        level = level_index.astype(jnp.float32)
        root = jnp.sqrt(jnp.maximum(level, 0.0) / FA)
        ladder[index * ROWS : (index + 1) * ROWS, :] = jnp.where(
            (level_index >= 1) & (level < cutoff), root * first, 0.0
        )
    sub_ladder = [second * math.sqrt(sub / FB) for sub in range(FB)]

    def start_of(component, half, level):
        segment, index = place_of(level)
        return (index + 1) * block + component * HALF + half * segments + segment

    for component in range(2):
        for half in range(halves):
            for tile in range(tiles):
                if tile < halo_tiles:
                    taken, place = left_ref, tile
                elif tile < halo_tiles + own_tiles:
                    taken, place = middle_ref, tile - halo_tiles
                else:
                    taken, place = right_ref, tile - halo_tiles - own_tiles
                turned = taken[component, half, :, place * LANES : (place + 1) * LANES].T
                for inner in range(levels_per_tile):
                    start = start_of(component, half, tile * levels_per_tile + inner)
                    source[pl.ds(start, FB, stride=ROWS), :] = turned[
                        inner * FB : (inner + 1) * FB
                    ]

    def fill_ghosts(buffer):
        for sub in range(FB):
            last = buffer[register(depth, sub), :]
            if mirrored:
                other = jnp.where(
                    segment_row == 0, pltpu.roll(last, ROWS - 1, 0), pltpu.roll(last, 1, 0)
                )
                buffer[register(depth + 1, sub), :] = other
            else:
                buffer[register(0, sub), :] = pltpu.roll(last, 1, 0)
                buffer[register(depth + 1, sub), :] = pltpu.roll(
                    buffer[register(1, sub), :], ROWS - 1, 0
                )

    if mirrored:
        for buffer in (even_buffer, odd_buffer):
            buffer[:block, :] = jnp.zeros((block, LANES), jnp.float32)

    terms = len(weights) - 1

    def begin(index, carry):
        for sub in range(FB):
            here = register(index, sub)
            value = source[here, :]
            swapped[here, :] = side * pltpu.roll(value, HALF, 0)
            even_buffer[here, :] = weights[terms] * value
        return carry

    lax.fori_loop(1, depth + 1, begin, 0)
    fill_ghosts(even_buffer)

    for order in range(terms - 1, -1, -1):
        target, present = (odd_buffer, even_buffer) if order % 2 else (even_buffer, odd_buffer)
        given = swapped if order % 2 else source

        def level_step(index, carry):
            lower = ladder[pl.ds(pl.multiple_of((index - 1) * ROWS, ROWS), ROWS), :]
            upper = ladder[pl.ds(pl.multiple_of(index * ROWS, ROWS), ROWS), :]
            centre = [present[register(index, sub), :] for sub in range(FB)]
            for sub in range(FB):
                here = register(index, sub)
                total = diagonal[register(index - 1, sub), :] * centre[sub]
                total += lower * present[register(index - 1, sub), :]
                total += upper * present[register(index + 1, sub), :]
                if sub > 0:
                    total += sub_ladder[sub] * centre[sub - 1]
                if sub + 1 < FB:
                    total += sub_ladder[sub + 1] * centre[sub + 1]
                if order == 0:
                    total = 0.5 * total
                addend = weights[order] * given[here, :]
                if order < terms - 1:
                    addend -= target[here, :]
                total += addend
                if order == 0:
                    turned = pltpu.roll(total, HALF, 0)
                    total = phase_real * total + phase_imag * (side * turned)
                target[here, :] = total
            return carry

        skipped = (terms - order) // 4 * 4 if mirrored else 0
        lax.fori_loop(1 + skipped, depth + 1, level_step, 0, unroll=4)
        if order > 0:
            fill_ghosts(target)

    for component in range(2):
        for half in range(halves):
            for level in range(own_tiles * levels_per_tile):
                start = start_of(component, half, level + halo_tiles * levels_per_tile)
                out_ref = out_refs[component * CUTS + level * FB // out_refs[0].shape[1]]
                first_row = level * FB % out_ref.shape[1]
                out_ref[half, first_row : first_row + FB, :] = even_buffer[
                    pl.ds(start, FB, stride=ROWS), :
                ]


def series_piece(scalars, cutoffs, sides, side_start, middle, first_group, groups, flip):
    width = middle.shape[3]
    left, right = sides
    halo = left.shape[3]
    halves = 2 if all(number % 2 == 0 for number in (first_group, groups, side_start)) else 1
    segments = HALF // halves
    depth = (width + 2 * halo) // FB // segments
    field = pltpu.VMEM(((depth + 2) * FB * ROWS, LANES), jnp.float32)
    first_unit, first_side = first_group // halves, side_start // halves
    return pl.pallas_call(
        functools.partial(series_kernel, series_weights(DEGREE), halves, flip, first_unit),
        grid=(groups // halves,),
        in_specs=[SCALARS] * len(scalars)
        + [
            pl.BlockSpec((1, GROUP * halves), lambda i: (0, i + first_unit)),
            pl.BlockSpec((2, halves, GROUP, halo), lambda i: (0, i + first_side, 0, 0)),
            pl.BlockSpec((2, halves, GROUP, width), lambda i: (0, i + first_unit, 0, 0)),
            pl.BlockSpec((2, halves, GROUP, halo), lambda i: (0, i + first_side, 0, 0)),
        ],
        out_specs=[pl.BlockSpec((halves, width // CUTS, GROUP), lambda i: (i, 0, 0))] * PARTS,
        out_shape=[jax.ShapeDtypeStruct((groups, width // CUTS, GROUP), jnp.float32)] * PARTS,
        scratch_shapes=[
            field,
            field,
            field,
            field,
            pltpu.VMEM(((depth + 1) * ROWS, LANES), jnp.float32),
            pltpu.VMEM((depth * FB * ROWS, LANES), jnp.float32),
        ],
        compiler_params=pltpu.CompilerParams(vmem_limit_bytes=VMEM_LIMIT),
        cost_estimate=NO_COST,
        name="series",
    )(*scalars, cutoffs, left, middle, right)


def mix_kernel(spin, cosines, sines, matrix_ref, *refs):
    own_refs, other_refs, out_refs = refs[:PARTS], refs[PARTS : 2 * PARTS], refs[2 * PARTS :]
    side = (2 * (lax.axis_index("spin") & 1) - 1).astype(jnp.float32)
    cosine = cosines[spin]
    sine = side * sines[spin]
    matrix = matrix_ref[...]
    length = own_refs[0].shape[1]
    for part in range(PARTS):
        component, cut = divmod(part, CUTS)
        mixed = lax.dot_general(
            matrix,
            cosine * own_refs[part][0] + sine * other_refs[part][0],
            (((1,), (1,)), ((), ())),
            precision=lax.Precision.HIGHEST,
            preferred_element_type=jnp.float32,
        )
        start = 0
        for out_ref in out_refs:
            stop = start + out_ref.shape[3]
            low, high = max(start, cut * length), min(stop, (cut + 1) * length)
            if low < high:
                out_ref[component, 0, :, low - start : high - start] = mixed[
                    :, low - cut * length : high - cut * length
                ]
            start = stop


def mix_piece(spin, cosines, sines, matrix, own, other, widths):
    groups, length = own[0].shape[:2]
    spec = pl.BlockSpec((1, length, GROUP), lambda i: (i, 0, 0))
    return pl.pallas_call(
        functools.partial(mix_kernel, spin),
        grid=(groups,),
        in_specs=[SCALARS, SCALARS, pl.BlockSpec((GROUP, GROUP), lambda i: (0, 0))]
        + [spec] * (2 * PARTS),
        out_specs=[pl.BlockSpec((2, 1, GROUP, width), lambda i: (0, i, 0, 0)) for width in widths],
        out_shape=[jax.ShapeDtypeStruct((2, groups, GROUP, width), jnp.float32) for width in widths],
        compiler_params=pltpu.CompilerParams(vmem_limit_bytes=VMEM_LIMIT),
        cost_estimate=NO_COST,
        name="mix",
    )(cosines, sines, matrix, *own, *other)


def join_kernel(counts, far_spin, cosines, sines, phase_ref, *refs):
    pieces = len(counts)
    own_refs, other_refs, out_ref = refs[:pieces], refs[pieces : 2 * pieces], refs[-1]
    groups = sum(counts)
    bits = groups.bit_length() - 1
    width = out_ref.shape[3]
    far_sine = (lax.axis_index("spin") & 2).astype(jnp.float32) * sines[far_spin] - sines[far_spin]
    places = [(piece, index) for piece in range(pieces) for index in range(counts[piece])]

    def row_tile(step, carry):
        rows = pl.ds(pl.multiple_of(step * ROWS, ROWS), ROWS)
        for lanes in range(width // LANES):
            columns = slice(lanes * LANES, (lanes + 1) * LANES)
            fields = []
            for component in range(2):
                field = [
                    cosines[far_spin] * own_refs[piece][component, index, rows, columns]
                    + far_sine * other_refs[piece][component, index, rows, columns]
                    for piece, index in places
                ]
                for bit in range(bits):
                    cosine, sine = cosines[LOW_BITS + bit], sines[LOW_BITS + bit]
                    following = list(field)
                    for group in range(groups):
                        if not (group >> bit) & 1:
                            partner = group | (1 << bit)
                            lower, upper = field[group], field[partner]
                            following[group] = cosine * lower - sine * upper
                            following[partner] = cosine * upper + sine * lower
                    field = following
                fields.append(field)
            for group in range(groups):
                entry = phase_ref[group, rows, :]
                phase_real = jnp.broadcast_to(entry[:, 0:1], (ROWS, LANES))
                phase_imag = jnp.broadcast_to(entry[:, 1:2], (ROWS, LANES))
                real, imag = fields[0][group], fields[1][group]
                out_ref[0, group, rows, columns] = phase_real * real + phase_imag * imag
                out_ref[1, group, rows, columns] = phase_real * imag - phase_imag * real
        return carry

    lax.fori_loop(0, out_ref.shape[2] // ROWS, row_tile, 0)


def join_chunk(far_spin, cosines, sines, table, own, other, target, start, width, out_shape):
    counts = [piece.shape[1] for piece in own]
    groups = sum(counts)
    depth = GROUP // 2
    chunk = start // width

    def spec(piece):
        place = chunk if piece.shape[3] > width else 0
        return pl.BlockSpec((2, piece.shape[1], depth, width), lambda i: (0, 0, i, place))

    operands = [cosines, sines, table, *own, *other]
    in_specs = [
        SCALARS,
        SCALARS,
        pl.BlockSpec((groups, depth, 8), lambda i: (0, i, 0)),
        *[spec(piece) for piece in [*own, *other]],
    ]
    aliases = {}
    if target is not None:
        aliases = {len(operands): 0}
        operands.append(target)
        in_specs.append(pl.BlockSpec(memory_space=pl.ANY))
    return pl.pallas_call(
        functools.partial(join_kernel, counts, far_spin),
        grid=(GROUP // depth,),
        in_specs=in_specs,
        out_specs=pl.BlockSpec((2, groups, depth, width), lambda i: (0, 0, i, chunk)),
        out_shape=jax.ShapeDtypeStruct(out_shape, jnp.float32),
        input_output_aliases=aliases,
        compiler_params=pltpu.CompilerParams(vmem_limit_bytes=VMEM_LIMIT),
        cost_estimate=NO_COST,
        name="join",
    )(*operands)


def partner_term(own_part, partner, cosine, sine_value, phase_bit, side_sign):
    keep_part = 1.0 - phase_bit
    real_part = cosine * own_part[0] + sine_value * (
        side_sign * phase_bit * partner[0] + keep_part * partner[1]
    )
    imag_part = cosine * own_part[1] + sine_value * (
        side_sign * phase_bit * partner[1] - keep_part * partner[0]
    )
    return jnp.stack([real_part, imag_part])


def piece_sizes(groups):
    if groups >= 16:
        unit = groups // 16
        sizes = [2 * unit, unit, unit, 2 * unit, 2 * unit, 2 * unit, 2 * unit]
    else:
        sizes = [2, 1, 1]
    return [*sizes, groups - sum(sizes)]


def halo_batches(count):
    batches = [1] * min(count, 4)
    while sum(batches) < count:
        batches.append(min(2, count - sum(batches)))
    return batches


def chunk_widths(width):
    wide = 2 * LANES
    return [wide] * (width // wide - 1) + [LANES, LANES]


def per_device(
    amplitudes,
    cutoffs,
    coupling_first,
    coupling_second,
    frozen_coupling,
    frozen_bits,
    drive_bits,
    angles,
):
    local_configs, width = amplitudes.shape[1:]
    groups = local_configs // GROUP
    local_bits = local_configs.bit_length() - 1
    halo = DEGREE * FB
    spin_count = lax.axis_size("spin")
    fock_count = lax.axis_size("fock")
    spin_place = lax.axis_index("spin")
    core_moves = [(i, i ^ 1) for i in range(spin_count)]
    far_moves = [(i, i ^ 2) for i in range(spin_count)]
    up = [(i, i + 1) for i in range(fock_count - 1)]
    down = [(j, i) for i, j in up]
    core_spin, far_spin = local_bits, local_bits + 1

    field = amplitudes.reshape(2, groups, GROUP, width)
    sizes = piece_sizes(groups)
    starts = [sum(sizes[:index]) for index in range(len(sizes))]
    raw_groups = sizes[0]
    raw = lax.ppermute(field[:, :raw_groups], "spin", far_moves)
    raw_cutoffs = lax.ppermute(cutoffs[: raw_groups * GROUP], "spin", far_moves).reshape(1, -1)
    cutoffs = cutoffs.reshape(1, -1)
    cosines, sines = jnp.cos(angles), jnp.sin(angles)
    matrix, phases = prepare(drive_bits, cosines, sines, local_configs)
    phases = phases.reshape(groups, GROUP, 8)
    others = (coupling_second, frozen_coupling, frozen_bits, drive_bits)

    pieces = [(field, cutoffs, start, size, 0) for start, size in zip(starts, sizes)]
    work = [*pieces[1:], (raw, raw_cutoffs, 0, raw_groups, 2), pieces[0]]
    last = len(pieces) - 2
    batches = halo_batches(last)
    batches += [1, 2]
    halos = []
    sent = []
    evolved = []
    crossed = []
    own, other = [], []

    def send_halo(*earlier):
        batch = work[len(halos) : len(halos) + batches[len(sent)]]
        edges = []
        for low, high in ((width - halo, width), (0, halo)):
            cuts = [source[:, start : start + size, :, low:high] for source, _, start, size, _ in batch]
            edges.append(jnp.concatenate(cuts, axis=1) if len(cuts) > 1 else cuts[0])
        if earlier:
            edges = lax.optimization_barrier((*edges, *earlier))[:2]
        sent.append((lax.ppermute(edges[0], "fock", up), lax.ppermute(edges[1], "fock", down)))
        place = 0
        for piece in batch:
            halos.append((sent[-1], place))
            place += piece[3]

    def series(*earlier):
        index = len(evolved)
        source, cuts, start, size, flip = work[index]
        scalars = (tied(coupling_first, *earlier), *others)
        piece = series_piece(scalars, cuts, *halos[index], source, start, size, flip)
        evolved.append(piece)
        crossed.append([lax.ppermute(part, "spin", core_moves) for part in piece])
        return piece[0]

    def mix(index, *earlier):
        widths = chunk_widths(width) if index == last else [width]
        cosine = tied(cosines, *earlier)
        mixed = mix_piece(
            core_spin, cosine, sines, matrix, evolved[index], crossed[index], widths
        )
        if index < last:
            own.append(mixed[0])
            other.append(lax.ppermute(mixed[0], "spin", far_moves))
        return mixed

    latest = matrix
    send_halo()
    prompt = min(4, last)
    for index in range(len(work)):
        waits = [latest]
        if index == 2:
            waits.append(raw)
        elif 2 < index < 6 and len(other) > index - 3:
            waits.append(other[index - 3])
        elif index > last and len(other) > index - 4:
            waits.append(other[index - 4])
        if len(sent) < len(batches):
            send_halo(*halos[index][0])
        latest = series(*waits)
        if index < prompt:
            latest = mix(index, latest)[0]
        elif prompt < index <= last + 1:
            last_pieces = mix(index - 1, latest)
            latest = last_pieces[0]
    (raw_other,) = mix(last + 1, latest)
    (raw_own,) = mix(last + 2, raw_other, other[-1])
    own, other = [raw_own, *own], [raw_other, *other]
    received = []
    result = None
    start = 0
    for chunk, piece in enumerate(last_pieces):
        going = piece if chunk < 2 else tied(piece, received[chunk - 2], raw_own)
        received.append(lax.ppermute(going, "spin", far_moves))
    for chunk, piece in enumerate(last_pieces):
        result = join_chunk(
            far_spin,
            cosines,
            sines,
            phases,
            [*own, piece],
            [*other, received[chunk]],
            result,
            start,
            piece.shape[3],
            field.shape,
        )
        start += piece.shape[3]
    result = result.reshape(amplitudes.shape)
    for bit in range(2, spin_count.bit_length() - 1):
        spin = local_bits + bit
        partner = lax.ppermute(result, "spin", [(i, i ^ (1 << bit)) for i in range(spin_count)])
        side = jnp.where((spin_place >> bit) & 1 == 1, 1.0, -1.0)
        result = partner_term(
            result, partner, cosines[spin], sines[spin], drive_bits[spin].astype(jnp.float32), side
        )
    return result


def solution(mesh):
    placed = (P(None, "spin", "fock"), P("spin"), P(), P(), P(), P(), P(), P())
    return jax.shard_map(
        per_device, mesh=mesh, in_specs=placed, out_specs=P(None, "spin", "fock"), check_vma=False
    )
```

time: 3100 us -> 513 us (0.17)
  other arithmetic: 1760 us -> 1.47 us
  local copies, waits for them, and re-layouts: 828 us -> 20.3 us
  Pallas kernels: 0 us -> 273 us
  blocking collectives: 186 us -> 0 us
  waiting for transfers between devices: 180 us -> 139 us
  starting transfers between devices: 110 us -> 71.4 us
    sub x15 -> x0, other arithmetic: 670 us -> none  [advance(): following = 2.0 * apply_operator(present) - previous]
    add x72 -> x0, other arithmetic: 569 us -> none  [the longest x15 277 us: advance(): total + weighted_term(following, real_weights[term_index], imag_weights[t...]
    slice x36 -> x6, local copies, waits for them, and re-layouts: 396 us -> 12.1 us  [the longest x4 8.97 us: send_halo(): source[:, start:start + size, :, low:high]]
    while x271 -> x0, local copies, waits for them, and re-layouts: 307 us -> none
    pallas_call x0 -> x24, Pallas kernels: none -> 273 us  [the longest x9 208 us: series_piece(): pl.pallas_call(functools.partial(series_kernel, series_weights(DEGREE), h...]
    neg x17 -> x0, other arithmetic: 205 us -> none  [weighted_term(): rotated = jnp.stack([-term_vector[1], term_vector[0]])]
    another operation x37 -> x0, other arithmetic: 191 us -> none  [rotate_bits(): vector = jnp.stack([new_lower, new_upper], axis=2).reshape(vector.shape)]
    all_to_all x1 -> x0, blocking collectives: 186 us -> none  [per_device(): lax.all_to_all(moved.reshape(2, spin_count, 1, rest, column_count), 'spin...]
  transfers between devices with their start and end apart: 33 -> 63, of which waited for: 1 -> 17; matrix products, arithmetic and copies ran while one was open for 17% -> 2% of each run, Pallas kernels for 0% -> 53%
where the time goes in v1:
time: 513 us; the launch traced here: 506 us
  Pallas kernels  273 us (53%)
  waiting for transfers between devices  139 us (27%)
  starting transfers between devices  71.4 us (14%)
  local copies, waits for them, and re-layouts  20.3 us (4%)
    pallas_call x9, Pallas kernels, series_piece(): pl.pallas_call(functools.partial(series_kernel, series_weights(DEGREE), h...  208 us
    ppermute x5, waiting for transfers between devices, per_device(): received.append(lax.ppermute(going, 'spin', far_moves))  50.6 us
    ppermute x7, starting transfers between devices, send_halo(): lax.ppermute(edges[1], 'fock', down)  37.2 us
    ppermute x7, waiting for transfers between devices, send_halo(): lax.ppermute(edges[1], 'fock', down)  36.6 us
    ppermute x6, waiting for transfers between devices, mix(): other.append(lax.ppermute(mixed[0], 'spin', far_moves))  35.2 us
    pallas_call x9, Pallas kernels, mix_piece(): pl.pallas_call(functools.partial(mix_kernel, spin), grid=(groups,), in_sp...  32.7 us
    pallas_call x5, Pallas kernels, join_chunk(): pl.pallas_call(functools.partial(join_kernel, counts, far_spin), grid=(GR...  28 us
    ppermute x7, waiting for transfers between devices, send_halo(): lax.ppermute(edges[0], 'fock', up)  10.8 us
  transfers between devices with their start and end apart: 63, of which 17 were waited for; matrix products, arithmetic and copies ran while one was open for 2% of the time, Pallas kernels for 53%

profile of v1, /device:TPU:26, one launch (start us, length us, event | category | flops | bytes accessed | tf_op | source)
XLA Modules:
  0.0 505.6 jit_solution(17509997656681422414)
XLA Ops:
  0.0 3.2 slice.74
  3.2 1.6 collective-permute-start.12
  7.4 4.6 collective-permute-start.1
  12.5 4.0 prepare.1
  16.6 3.7 collective-permute-done.1.right_ref
  21.6 5.0 collective-permute-start.7
  26.7 13.5 %series.9 = (f32[1,512,128]{2,1,0:T(8,128)S(1)}, f32[1,512,128]{2,1,0:T(8,128)S(1)}, f32[1,512,128]{2,1,0:T(8,128)S(1)}, f32[1,512,128]{2,1,0:T(8,128)S(1)}) custom-call(f32[13]{0:T(128)S(1)} %copy-done.17, f32[13]{0:T(128)S(1)} %copy-done.18, f32[16]{0:T(128)S(1)} %copy-done.19, s32[16]{0:T(128)S(1)} %copy-done.20, s32[13]{0:T(128)S(1)} %copy-done.16, ...), custom_call_target="tpu_custom_call" | custom-call | flops 1 | bytes 1 | tf_op jit(solution)/shard_map/series/pallas_call | solution.py:314
  40.8 2.1 fusion
  44.2 5.5 %collective-permute-start.14 = (f32[2,2,128,256]{3,2,1,0:T(8,128)S(1)}, f32[2,2,128,256]{3,2,1,0:T(8,128)S(1)}, u32[]{:S(2)}, u32[]{:S(2)}) collective-permute-start(f32[2,2,128,256]{3,2,1,0:T(8,128)S(1)} %get-tuple-element.99), channel_id=1, source_target_pairs={{1,0},{2,1},{3,2},{4,3},{5,4},{6,5},{7,6},{9,8},{10,9},{11,10},{12... | collective-permute-start | bytes 1572872 | tf_op jit(solution)/shard_map/ppermute | solution.py:547
  53.3 13.5 %series.10 = (f32[1,512,128]{2,1,0:T(8,128)S(1)}, f32[1,512,128]{2,1,0:T(8,128)S(1)}, f32[1,512,128]{2,1,0:T(8,128)S(1)}, f32[1,512,128]{2,1,0:T(8,128)S(1)}) custom-call(f32[13]{0:T(128)S(1)} %copy-done.17, f32[13]{0:T(128)S(1)} %copy-done.18, f32[16]{0:T(128)S(1)} %copy-done.19, s32[16]{0:T(128)S(1)} %copy-done.20, s32[13]{0:T(128)S(1)} %copy-done.16, ...), custom_call_target="tpu_custom_call" | custom-call | flops 1 | bytes 1 | tf_op jit(solution)/shard_map/series/pallas_call | solution.py:314
  67.0 4.3 collective-permute-done.14.right_ref
  74.2 5.5 %collective-permute-start.21 = (f32[2,2,128,256]{3,2,1,0:T(8,128)S(1)}, f32[2,2,128,256]{3,2,1,0:T(8,128)S(1)}, u32[]{:S(2)}, u32[]{:S(2)}) collective-permute-start(f32[2,2,128,256]{3,2,1,0:T(8,128)S(1)} %get-tuple-element.107), channel_id=1, source_target_pairs={{1,0},{2,1},{3,2},{4,3},{5,4},{6,5},{7,6},{9,8},{10,9},{11,10},{12... | collective-permute-start | bytes 1572872 | tf_op jit(solution)/shard_map/ppermute | solution.py:547
  81.3 22.9 %series.11 = (f32[2,512,128]{2,1,0:T(8,128)S(1)}, f32[2,512,128]{2,1,0:T(8,128)S(1)}, f32[2,512,128]{2,1,0:T(8,128)S(1)}, f32[2,512,128]{2,1,0:T(8,128)S(1)}) custom-call(f32[13]{0:T(128)S(1)} %copy-done.17, f32[13]{0:T(128)S(1)} %copy-done.18, f32[16]{0:T(128)S(1)} %copy-done.19, s32[16]{0:T(128)S(1)} %copy-done.20, s32[13]{0:T(128)S(1)} %copy-done.16, ...), custom_call_target="tpu_custom_call" | custom-call | flops 1 | bytes 1 | tf_op jit(solution)/shard_map/series/pallas_call | solution.py:314
  105.4 4.3 fusion.1
  111.2 5.5 %collective-permute-start.28 = (f32[2,4,128,256]{3,2,1,0:T(8,128)}, f32[2,4,128,256]{3,2,1,0:T(8,128)S(1)}, u32[]{:S(2)}, u32[]{:S(2)}) collective-permute-start(f32[2,4,128,256]{3,2,1,0:T(8,128)} %get-tuple-element.115), channel_id=1, source_target_pairs={{1,0},{2,1},{3,2},{4,3},{5,4},{6,5},{7,6},{9,8},{10,9},{11,10},{12... | collective-permute-start | bytes 3145736 | tf_op jit(solution)/shard_map/ppermute | solution.py:547
  116.7 1.6 collective-permute-start.26
  118.3 3.6 mix.11.refs_3_
  122.5 7.9 %collective-permute-done.19.refs_9_ = f32[2,1,128,1024]{3,2,1,0:T(8,128)S(1)} collective-permute-done((f32[2,1,128,1024]{3,2,1,0:T(8,128)S(1)}, f32[2,1,128,1024]{3,2,1,0:T(8,128)S(1)}, u32[]{:S(2)}, u32[]{:S(2)}) %collective-permute-start.19) | collective-permute-done | bytes 1048608 | tf_op jit(solution)/shard_map/ppermute | solution.py:570
  130.3 22.9 %series.12 = (f32[2,512,128]{2,1,0:T(8,128)S(1)}, f32[2,512,128]{2,1,0:T(8,128)S(1)}, f32[2,512,128]{2,1,0:T(8,128)S(1)}, f32[2,512,128]{2,1,0:T(8,128)S(1)}) custom-call(f32[13]{0:T(128)S(1)} %copy-done.17, f32[13]{0:T(128)S(1)} %copy-done.18, f32[16]{0:T(128)S(1)} %copy-done.19, s32[16]{0:T(128)S(1)} %copy-done.20, s32[13]{0:T(128)S(1)} %copy-done.16, ...), custom_call_target="tpu_custom_call" | custom-call | flops 1 | bytes 1 | tf_op jit(solution)/shard_map/series/pallas_call | solution.py:314
  155.1 5.8 %collective-permute-done.28.right_ref = f32[2,4,128,256]{3,2,1,0:T(8,128)S(1)} collective-permute-done((f32[2,4,128,256]{3,2,1,0:T(8,128)}, f32[2,4,128,256]{3,2,1,0:T(8,128)S(1)}, u32[]{:S(2)}, u32[]{:S(2)}) %collective-permute-start.28) | collective-permute-done | bytes 1048608 | tf_op jit(solution)/shard_map/ppermute | solution.py:547
  165.1 6.7 %collective-permute-start.35 = (f32[2,4,128,256]{3,2,1,0:T(8,128)}, f32[2,4,128,256]{3,2,1,0:T(8,128)}, u32[]{:S(2)}, u32[]{:S(2)}) collective-permute-start(f32[2,4,128,256]{3,2,1,0:T(8,128)} %get-tuple-element.125), channel_id=1, source_target_pairs={{1,0},{2,1},{3,2},{4,3},{5,4},{6,5},{7,6},{9,8},{10,9},{11,10},{12... | collective-permute-start | bytes 3145736 | tf_op jit(solution)/shard_map/ppermute | solution.py:547
  172.0 1.7 collective-permute-done.25.refs_7_
  175.3 3.6 mix.12.refs_4_
  178.9 22.9 %series.13 = (f32[2,512,128]{2,1,0:T(8,128)S(1)}, f32[2,512,128]{2,1,0:T(8,128)S(1)}, f32[2,512,128]{2,1,0:T(8,128)S(1)}, f32[2,512,128]{2,1,0:T(8,128)S(1)}) custom-call(f32[13]{0:T(128)S(1)} %copy-done.17, f32[13]{0:T(128)S(1)} %copy-done.18, f32[16]{0:T(128)S(1)} %copy-done.19, s32[16]{0:T(128)S(1)} %copy-done.20, s32[13]{0:T(128)S(1)} %copy-done.16, ...), custom_call_target="tpu_custom_call" | custom-call | flops 1 | bytes 1 | tf_op jit(solution)/shard_map/series/pallas_call | solution.py:314
  202.4 10.7 %collective-permute-done.34.left_ref = f32[2,4,128,256]{3,2,1,0:T(8,128)S(1)} collective-permute-done((f32[2,4,128,256]{3,2,1,0:T(8,128)}, f32[2,4,128,256]{3,2,1,0:T(8,128)S(1)}, u32[]{:S(2)}, u32[]{:S(2)}) %collective-permute-start.34) | collective-permute-done | bytes 1048608 | tf_op jit(solution)/shard_map/ppermute | solution.py:547
  213.2 22.7 %collective-permute-done.35.right_ref = f32[2,4,128,256]{3,2,1,0:T(8,128)} collective-permute-done((f32[2,4,128,256]{3,2,1,0:T(8,128)}, f32[2,4,128,256]{3,2,1,0:T(8,128)}, u32[]{:S(2)}, u32[]{:S(2)}) %collective-permute-start.35) | collective-permute-done | bytes 1048608 | tf_op jit(solution)/shard_map/ppermute | solution.py:547
  237.8 22.9 %series.14 = (f32[2,512,128]{2,1,0:T(8,128)S(1)}, f32[2,512,128]{2,1,0:T(8,128)S(1)}, f32[2,512,128]{2,1,0:T(8,128)S(1)}, f32[2,512,128]{2,1,0:T(8,128)S(1)}) custom-call(f32[13]{0:T(128)S(1)} %copy-done.17, f32[13]{0:T(128)S(1)} %copy-done.18, f32[16]{0:T(128)S(1)} %copy-done.19, s32[16]{0:T(128)S(1)} %copy-done.20, s32[13]{0:T(128)S(1)} %copy-done.16, ...), custom_call_target="tpu_custom_call" | custom-call | flops 1 | bytes 1 | tf_op jit(solution)/shard_map/series/pallas_call | solution.py:314
  261.3 4.4 collective-permute-start.43
  265.8 3.9 mix.13.refs_5_
  269.7 43.0 %series.15 = (f32[4,512,128]{2,1,0:T(8,128)S(1)}, f32[4,512,128]{2,1,0:T(8,128)S(1)}, f32[4,512,128]{2,1,0:T(8,128)S(1)}, f32[4,512,128]{2,1,0:T(8,128)S(1)}) custom-call(f32[13]{0:T(128)S(1)} %copy-done.17, f32[13]{0:T(128)S(1)} %copy-done.18, f32[16]{0:T(128)S(1)} %copy-done.19, s32[16]{0:T(128)S(1)} %copy-done.20, s32[13]{0:T(128)S(1)} %copy-done.16, ...), custom_call_target="tpu_custom_call" | custom-call | flops 1 | bytes 1 | tf_op jit(solution)/shard_map/series/pallas_call | solution.py:314
  317.8 4.1 mix.14.refs_6_
  321.9 1.6 collective-permute-start.53
  324.1 22.9 %series.16 = (f32[2,512,128]{2,1,0:T(8,128)S(1)}, f32[2,512,128]{2,1,0:T(8,128)S(1)}, f32[2,512,128]{2,1,0:T(8,128)S(1)}, f32[2,512,128]{2,1,0:T(8,128)S(1)}) custom-call(f32[13]{0:T(128)S(1)} %copy-done.17, f32[13]{0:T(128)S(1)} %copy-done.18, f32[16]{0:T(128)S(1)} %copy-done.19, s32[16]{0:T(128)S(1)} %copy-done.20, s32[13]{0:T(128)S(1)} %copy-done.16, ...), custom_call_target="tpu_custom_call" | custom-call | flops 1 | bytes 1 | tf_op jit(solution)/shard_map/series/pallas_call | solution.py:314
  349.3 6.3 %mix.15 = (f32[2,4,128,256]{3,2,1,0:T(8,128)S(1)}, f32[2,4,128,256]{3,2,1,0:T(8,128)S(1)}, f32[2,4,128,256]{3,2,1,0:T(8,128)S(1)}, f32[2,4,128,128]{3,2,1,0:T(8,128)S(1)}, f32[2,4,128,128]{3,2,1,0:T(8,128)S(1)}) custom-call(f32[13]{0:T(128)S(1)} %copy-done.15, f32[13]{0:T(128)S(1)} %copy-done.14, f32[128,128]{1,0:T(8,128)S(1)} %copy-done.1, ...), custom_call_target="tpu_custom_call" | custom-call | flops 1 | bytes 1 | tf_op jit(solution)/shard_map/mix/pallas_call | solution.py:370
  355.6 7.8 %collective-permute-done.48.refs_13_ = f32[2,2,128,1024]{3,2,1,0:T(8,128)} collective-permute-done((f32[2,2,128,1024]{3,2,1,0:T(8,128)}, f32[2,2,128,1024]{3,2,1,0:T(8,128)}, u32[]{:S(2)}, u32[]{:S(2)}) %collective-permute-start.48) | collective-permute-done | bytes 2097184 | tf_op jit(solution)/shard_map/ppermute | solution.py:570
  364.9 23.2 %series.17 = (f32[2,512,128]{2,1,0:T(8,128)S(1)}, f32[2,512,128]{2,1,0:T(8,128)S(1)}, f32[2,512,128]{2,1,0:T(8,128)S(1)}, f32[2,512,128]{2,1,0:T(8,128)S(1)}) custom-call(f32[13]{0:T(128)S(1)} %copy-done.17, f32[13]{0:T(128)S(1)} %copy-done.18, f32[16]{0:T(128)S(1)} %copy-done.19, s32[16]{0:T(128)S(1)} %copy-done.20, s32[13]{0:T(128)S(1)} %copy-done.16, ...), custom_call_target="tpu_custom_call" | custom-call | flops 1 | bytes 1 | tf_op jit(solution)/shard_map/series/pallas_call | solution.py:314
  388.8 19.5 %collective-permute-done.53.refs_14_ = f32[2,2,128,1024]{3,2,1,0:T(8,128)} collective-permute-done((f32[2,2,128,1024]{3,2,1,0:T(8,128)}, f32[2,2,128,1024]{3,2,1,0:T(8,128)}, u32[]{:S(2)}, u32[]{:S(2)}) %collective-permute-start.53) | collective-permute-done | bytes 2097184 | tf_op jit(solution)/shard_map/ppermute | solution.py:570
  408.3 4.1 mix.16.refs_8_
  412.4 1.6 collective-permute-start.61
  417.9 4.1 mix.17.refs_0_
  422.0 8.8 %collective-permute-done.58.refs_15_ = f32[2,4,128,256]{3,2,1,0:T(8,128)} collective-permute-done((f32[2,4,128,256]{3,2,1,0:T(8,128)S(1)}, f32[2,4,128,256]{3,2,1,0:T(8,128)}, u32[]{:S(2)}, u32[]{:S(2)}) %collective-permute-start.58) | collective-permute-done | bytes 1048608 | tf_op jit(solution)/shard_map/ppermute | solution.py:600
  432.3 20.8 %collective-permute-done.61.refs_15_ = f32[2,4,128,256]{3,2,1,0:T(8,128)S(1)} collective-permute-done((f32[2,4,128,256]{3,2,1,0:T(8,128)S(1)}, f32[2,4,128,256]{3,2,1,0:T(8,128)S(1)}, u32[]{:S(2)}, u32[]{:S(2)}) %collective-permute-start.61) | collective-permute-done | bytes 1048608 | tf_op jit(solution)/shard_map/ppermute | solution.py:600
  454.7 20.9 %collective-permute-done.59.refs_15_ = f32[2,4,128,256]{3,2,1,0:T(8,128)S(1)} collective-permute-done((f32[2,4,128,256]{3,2,1,0:T(8,128)S(1)}, f32[2,4,128,256]{3,2,1,0:T(8,128)S(1)}, u32[]{:S(2)}, u32[]{:S(2)}) %collective-permute-start.59) | collective-permute-done | bytes 1048608 | tf_op jit(solution)/shard_map/ppermute | solution.py:600
  477.1 6.4 %join.5.refs_16_ = f32[2,16,128,1024]{3,2,1,0:T(8,128)} custom-call(f32[13]{0:T(128)S(1)} %copy-done.15, f32[13]{0:T(128)S(1)} %copy-done.14, f32[16,128,8]{2,1,0:T(8,128)S(1)} %bitcast.5, f32[2,2,128,1024]{3,2,1,0:T(8,128)} %mix.17.refs_0_, f32[2,1,128,1024]{3,2,1,0:T(8,128)S(1)} %mix.9.refs_1_, f32[2,1,128,1024]{3,2,1,0:T(8,128)S(1)} %mix.10.refs_2_, ...), custom_call_target="tpu_custom_call" | custom-call | flops 1 | bytes 1 | tf_op jit(solution)/shard_map/join/pallas_call | solution.py:448
  483.5 6.4 %join.6.refs_16_ = f32[2,16,128,1024]{3,2,1,0:T(8,128)} custom-call(f32[13]{0:T(128)S(1)} %copy-done.15, f32[13]{0:T(128)S(1)} %copy-done.14, f32[16,128,8]{2,1,0:T(8,128)S(1)} %bitcast.6, f32[2,2,128,1024]{3,2,1,0:T(8,128)} %mix.17.refs_0_, f32[2,1,128,1024]{3,2,1,0:T(8,128)S(1)} %mix.9.refs_1_, ...), custom_call_target="tpu_custom_call", output_to_operand_aliasing={{}: (19, {})} | custom-call | flops 1 | bytes 1 | tf_op jit(solution)/shard_map/join/pallas_call | solution.py:448
  489.9 6.4 %join.7.refs_16_ = f32[2,16,128,1024]{3,2,1,0:T(8,128)} custom-call(f32[13]{0:T(128)S(1)} %copy-done.15, f32[13]{0:T(128)S(1)} %copy-done.14, f32[16,128,8]{2,1,0:T(8,128)S(1)} %bitcast.7, f32[2,2,128,1024]{3,2,1,0:T(8,128)} %mix.17.refs_0_, f32[2,1,128,1024]{3,2,1,0:T(8,128)S(1)} %mix.9.refs_1_, ...), custom_call_target="tpu_custom_call", output_to_operand_aliasing={{}: (19, {})} | custom-call | flops 1 | bytes 1 | tf_op jit(solution)/shard_map/join/pallas_call | solution.py:448
  496.4 4.4 join.8.refs_16_
  500.8 4.4 join.9
  (168 shorter events, 47.1 us)
Async XLA Ops:
  3.2 78.1 %collective-permute-start.12 = (f32[2,2,128,1024]{3,2,1,0:T(8,128)}, f32[2,2,128,1024]{3,2,1,0:T(8,128)}, u32[]{:S(2)}, u32[]{:S(2)}) collective-permute-start(f32[2,2,128,1024]{3,2,1,0:T(8,128)} %slice.74), channel_id=1, source_target_pairs={{0,16},{8,24},{16,0},{24,8},{1,17},{9,25},{17,1},{25,9},{2,18},{10... | collective-permute-start | bytes 6291464 | tf_op jit(solution)/shard_map/ppermute | solution.py:520
  6.1 10.5 %collective-permute-start = (f32[2,1,128,256]{3,2,1,0:T(8,128)S(1)}, f32[2,1,128,256]{3,2,1,0:T(8,128)S(1)}, u32[]{:S(2)}, u32[]{:S(2)}) collective-permute-start(f32[2,1,128,256]{3,2,1,0:T(8,128)S(1)} %get-tuple-element.170), channel_id=1, source_target_pairs={{0,1},{1,2},{2,3},{3,4},{4,5},{5,6},{6,7},{8,9},{9,10},{10,11},{11... | collective-permute-start | bytes 786440 | tf_op jit(solution)/shard_map/ppermute | solution.py:547
  7.4 12.9 %collective-permute-start.1 = (f32[2,1,128,256]{3,2,1,0:T(8,128)S(1)}, f32[2,1,128,256]{3,2,1,0:T(8,128)S(1)}, u32[]{:S(2)}, u32[]{:S(2)}) collective-permute-start(f32[2,1,128,256]{3,2,1,0:T(8,128)S(1)} %get-tuple-element.169), channel_id=1, source_target_pairs={{1,0},{2,1},{3,2},{4,3},{5,4},{6,5},{7,6},{9,8},{10,9},{11,10},{12... | collective-permute-start | bytes 786440 | tf_op jit(solution)/shard_map/ppermute | solution.py:547
  20.3 22.6 %collective-permute-start.6 = (f32[2,1,128,256]{3,2,1,0:T(8,128)S(1)}, f32[2,1,128,256]{3,2,1,0:T(8,128)S(1)}, u32[]{:S(2)}, u32[]{:S(2)}) collective-permute-start(f32[2,1,128,256]{3,2,1,0:T(8,128)S(1)} %get-tuple-element.90), channel_id=1, source_target_pairs={{0,1},{1,2},{2,3},{3,4},{4,5},{5,6},{6,7},{8,9},{9,10},{10,11},{11... | collective-permute-start | bytes 786440 | tf_op jit(solution)/shard_map/ppermute | solution.py:547
  21.6 21.3 %collective-permute-start.7 = (f32[2,1,128,256]{3,2,1,0:T(8,128)S(1)}, f32[2,1,128,256]{3,2,1,0:T(8,128)S(1)}, u32[]{:S(2)}, u32[]{:S(2)}) collective-permute-start(f32[2,1,128,256]{3,2,1,0:T(8,128)S(1)} %get-tuple-element.91), channel_id=1, source_target_pairs={{1,0},{2,1},{3,2},{4,3},{5,4},{6,5},{7,6},{9,8},{10,9},{11,10},{12... | collective-permute-start | bytes 786440 | tf_op jit(solution)/shard_map/ppermute | solution.py:547
  42.9 24.1 %collective-permute-start.13 = (f32[2,2,128,256]{3,2,1,0:T(8,128)S(1)}, f32[2,2,128,256]{3,2,1,0:T(8,128)S(1)}, u32[]{:S(2)}, u32[]{:S(2)}) collective-permute-start(f32[2,2,128,256]{3,2,1,0:T(8,128)S(1)} %get-tuple-element.98), channel_id=1, source_target_pairs={{0,1},{1,2},{2,3},{3,4},{4,5},{5,6},{6,7},{8,9},{9,10},{10,11},{11... | collective-permute-start | bytes 1572872 | tf_op jit(solution)/shard_map/ppermute | solution.py:547
  44.2 27.1 %collective-permute-start.14 = (f32[2,2,128,256]{3,2,1,0:T(8,128)S(1)}, f32[2,2,128,256]{3,2,1,0:T(8,128)S(1)}, u32[]{:S(2)}, u32[]{:S(2)}) collective-permute-start(f32[2,2,128,256]{3,2,1,0:T(8,128)S(1)} %get-tuple-element.99), channel_id=1, source_target_pairs={{1,0},{2,1},{3,2},{4,3},{5,4},{6,5},{7,6},{9,8},{10,9},{11,10},{12... | collective-permute-start | bytes 1572872 | tf_op jit(solution)/shard_map/ppermute | solution.py:547
  71.3 33.7 %collective-permute-start.20 = (f32[2,2,128,256]{3,2,1,0:T(8,128)S(1)}, f32[2,2,128,256]{3,2,1,0:T(8,128)S(1)}, u32[]{:S(2)}, u32[]{:S(2)}) collective-permute-start(f32[2,2,128,256]{3,2,1,0:T(8,128)S(1)} %get-tuple-element.106), channel_id=1, source_target_pairs={{0,1},{1,2},{2,3},{3,4},{4,5},{5,6},{6,7},{8,9},{9,10},{10,11},{11... | collective-permute-start | bytes 1572872 | tf_op jit(solution)/shard_map/ppermute | solution.py:547
  74.2 35.5 %collective-permute-start.21 = (f32[2,2,128,256]{3,2,1,0:T(8,128)S(1)}, f32[2,2,128,256]{3,2,1,0:T(8,128)S(1)}, u32[]{:S(2)}, u32[]{:S(2)}) collective-permute-start(f32[2,2,128,256]{3,2,1,0:T(8,128)S(1)} %get-tuple-element.107), channel_id=1, source_target_pairs={{1,0},{2,1},{3,2},{4,3},{5,4},{6,5},{7,6},{9,8},{10,9},{11,10},{12... | collective-permute-start | bytes 1572872 | tf_op jit(solution)/shard_map/ppermute | solution.py:547
  104.3 26.0 %collective-permute-start.19 = (f32[2,1,128,1024]{3,2,1,0:T(8,128)S(1)}, f32[2,1,128,1024]{3,2,1,0:T(8,128)S(1)}, u32[]{:S(2)}, u32[]{:S(2)}) collective-permute-start(f32[2,1,128,1024]{3,2,1,0:T(8,128)S(1)} %mix.9.refs_1_), channel_id=1, source_target_pairs={{0,16},{8,24},{16,0},{24,8},{1,17},{9,25},{17,1},{25,9},{2,18},{10... | collective-permute-start | bytes 3145736 | tf_op jit(solution)/shard_map/ppermute | solution.py:570
  105.0 11.7 %collective-permute-start.17 = (f32[2,512,128]{2,1,0:T(8,128)S(1)}, f32[2,512,128]{2,1,0:T(8,128)S(1)}, u32[]{:S(2)}, u32[]{:S(2)}) collective-permute-start(f32[2,512,128]{2,1,0:T(8,128)S(1)} %get-tuple-element.103.refs_2_), channel_id=1, source_target_pairs={{0,8},{8,0},{16,24},{24,16},{1,9},{9,1},{17,25},{25,17},{2,10},{10... | collective-permute-start | bytes 1572872 | tf_op jit(solution)/shard_map/ppermute | solution.py:559
  109.7 43.6 %collective-permute-start.27 = (f32[2,4,128,256]{3,2,1,0:T(8,128)}, f32[2,4,128,256]{3,2,1,0:T(8,128)S(1)}, u32[]{:S(2)}, u32[]{:S(2)}) collective-permute-start(f32[2,4,128,256]{3,2,1,0:T(8,128)} %get-tuple-element.114), channel_id=1, source_target_pairs={{0,1},{1,2},{2,3},{3,4},{4,5},{5,6},{6,7},{8,9},{9,10},{10,11},{11... | collective-permute-start | bytes 3145736 | tf_op jit(solution)/shard_map/ppermute | solution.py:547
  111.2 49.7 %collective-permute-start.28 = (f32[2,4,128,256]{3,2,1,0:T(8,128)}, f32[2,4,128,256]{3,2,1,0:T(8,128)S(1)}, u32[]{:S(2)}, u32[]{:S(2)}) collective-permute-start(f32[2,4,128,256]{3,2,1,0:T(8,128)} %get-tuple-element.115), channel_id=1, source_target_pairs={{1,0},{2,1},{3,2},{4,3},{5,4},{6,5},{7,6},{9,8},{10,9},{11,10},{12... | collective-permute-start | bytes 3145736 | tf_op jit(solution)/shard_map/ppermute | solution.py:547
  116.7 45.7 %collective-permute-start.26 = (f32[2,1,128,1024]{3,2,1,0:T(8,128)S(1)}, f32[2,1,128,1024]{3,2,1,0:T(8,128)S(1)}, u32[]{:S(2)}, u32[]{:S(2)}) collective-permute-start(f32[2,1,128,1024]{3,2,1,0:T(8,128)S(1)} %mix.10.refs_2_), channel_id=1, source_target_pairs={{0,16},{8,24},{16,0},{24,8},{1,17},{9,25},{17,1},{25,9},{2,18},{10... | collective-permute-start | bytes 3145736 | tf_op jit(solution)/shard_map/ppermute | solution.py:570
  121.9 114.0 %collective-permute-start.29 = (f32[2,2,128,1024]{3,2,1,0:T(8,128)}, f32[2,2,128,1024]{3,2,1,0:T(8,128)S(1)}, u32[]{:S(2)}, u32[]{:S(2)}) collective-permute-start(f32[2,2,128,1024]{3,2,1,0:T(8,128)} %mix.11.refs_3_), channel_id=1, source_target_pairs={{0,16},{8,24},{16,0},{24,8},{1,17},{9,25},{17,1},{25,9},{2,18},{10... | collective-permute-start | bytes 6291464 | tf_op jit(solution)/shard_map/ppermute | solution.py:570
  153.2 10.5 %collective-permute-start.22 = (f32[2,512,128]{2,1,0:T(8,128)S(1)}, f32[2,512,128]{2,1,0:T(8,128)S(1)}, u32[]{:S(2)}, u32[]{:S(2)}) collective-permute-start(f32[2,512,128]{2,1,0:T(8,128)S(1)} %get-tuple-element.108.refs_0_), channel_id=1, source_target_pairs={{0,8},{8,0},{16,24},{24,16},{1,9},{9,1},{17,25},{25,17},{2,10},{10... | collective-permute-start | bytes 1572872 | tf_op jit(solution)/shard_map/ppermute | solution.py:559
  153.3 11.7 %collective-permute-start.23 = (f32[2,512,128]{2,1,0:T(8,128)S(1)}, f32[2,512,128]{2,1,0:T(8,128)S(1)}, u32[]{:S(2)}, u32[]{:S(2)}) collective-permute-start(f32[2,512,128]{2,1,0:T(8,128)S(1)} %get-tuple-element.110.refs_1_), channel_id=1, source_target_pairs={{0,8},{8,0},{16,24},{24,16},{1,9},{9,1},{17,25},{25,17},{2,10},{10... | collective-permute-start | bytes 1572872 | tf_op jit(solution)/shard_map/ppermute | solution.py:559
  160.9 10.8 %collective-permute-start.24 = (f32[2,512,128]{2,1,0:T(8,128)S(1)}, f32[2,512,128]{2,1,0:T(8,128)S(1)}, u32[]{:S(2)}, u32[]{:S(2)}) collective-permute-start(f32[2,512,128]{2,1,0:T(8,128)S(1)} %get-tuple-element.111.refs_2_), channel_id=1, source_target_pairs={{0,8},{8,0},{16,24},{24,16},{1,9},{9,1},{17,25},{25,17},{2,10},{10... | collective-permute-start | bytes 1572872 | tf_op jit(solution)/shard_map/ppermute | solution.py:559
  162.4 40.0 %collective-permute-start.42 = (f32[2,4,128,256]{3,2,1,0:T(8,128)}, f32[2,4,128,256]{3,2,1,0:T(8,128)S(1)}, u32[]{:S(2)}, u32[]{:S(2)}) collective-permute-start(f32[2,4,128,256]{3,2,1,0:T(8,128)} %get-tuple-element.132), channel_id=1, source_target_pairs={{0,1},{1,2},{2,3},{3,4},{4,5},{5,6},{6,7},{8,9},{9,10},{10,11},{11... | collective-permute-start | bytes 3145736 | tf_op jit(solution)/shard_map/ppermute | solution.py:547
  163.7 49.4 %collective-permute-start.34 = (f32[2,4,128,256]{3,2,1,0:T(8,128)}, f32[2,4,128,256]{3,2,1,0:T(8,128)S(1)}, u32[]{:S(2)}, u32[]{:S(2)}) collective-permute-start(f32[2,4,128,256]{3,2,1,0:T(8,128)} %get-tuple-element.124), channel_id=1, source_target_pairs={{0,1},{1,2},{2,3},{3,4},{4,5},{5,6},{6,7},{8,9},{9,10},{10,11},{11... | collective-permute-start | bytes 3145736 | tf_op jit(solution)/shard_map/ppermute | solution.py:547
  165.1 70.8 %collective-permute-start.35 = (f32[2,4,128,256]{3,2,1,0:T(8,128)}, f32[2,4,128,256]{3,2,1,0:T(8,128)}, u32[]{:S(2)}, u32[]{:S(2)}) collective-permute-start(f32[2,4,128,256]{3,2,1,0:T(8,128)} %get-tuple-element.125), channel_id=1, source_target_pairs={{1,0},{2,1},{3,2},{4,3},{5,4},{6,5},{7,6},{9,8},{10,9},{11,10},{12... | collective-permute-start | bytes 3145736 | tf_op jit(solution)/shard_map/ppermute | solution.py:547
  173.8 28.1 %collective-permute-start.41 = (s32[256]{0:T(256)S(1)}, s32[256]{0:T(256)S(1)}, u32[]{:S(2)}, u32[]{:S(2)}) collective-permute-start(s32[256]{0:T(256)S(1)} %slice.65), channel_id=1, source_target_pairs={{0,16},{8,24},{16,0},{24,8},{1,17},{9,25},{17,1},{25,9},{2,18},{10... | collective-permute-start | bytes 3080 | tf_op jit(solution)/shard_map/ppermute | solution.py:521
  201.8 121.6 %collective-permute-start.40 = (f32[2,2,128,1024]{3,2,1,0:T(8,128)}, f32[2,2,128,1024]{3,2,1,0:T(8,128)}, u32[]{:S(2)}, u32[]{:S(2)}) collective-permute-start(f32[2,2,128,1024]{3,2,1,0:T(8,128)} %mix.12.refs_4_), channel_id=1, source_target_pairs={{0,16},{8,24},{16,0},{24,8},{1,17},{9,25},{17,1},{25,9},{2,18},{10... | collective-permute-start | bytes 6291464 | tf_op jit(solution)/shard_map/ppermute | solution.py:570
  202.4 58.3 %collective-permute-start.30 = (f32[2,512,128]{2,1,0:T(8,128)S(1)}, f32[2,512,128]{2,1,0:T(8,128)S(1)}, u32[]{:S(2)}, u32[]{:S(2)}) collective-permute-start(f32[2,512,128]{2,1,0:T(8,128)S(1)} %get-tuple-element.116.refs_0_), channel_id=1, source_target_pairs={{0,8},{8,0},{16,24},{24,16},{1,9},{9,1},{17,25},{25,17},{2,10},{10... | collective-permute-start | bytes 1572872 | tf_op jit(solution)/shard_map/ppermute | solution.py:559
  213.2 47.7 %collective-permute-start.31 = (f32[2,512,128]{2,1,0:T(8,128)S(1)}, f32[2,512,128]{2,1,0:T(8,128)S(1)}, u32[]{:S(2)}, u32[]{:S(2)}) collective-permute-start(f32[2,512,128]{2,1,0:T(8,128)S(1)} %get-tuple-element.120.refs_1_), channel_id=1, source_target_pairs={{0,8},{8,0},{16,24},{24,16},{1,9},{9,1},{17,25},{25,17},{2,10},{10... | collective-permute-start | bytes 1572872 | tf_op jit(solution)/shard_map/ppermute | solution.py:559
  235.9 25.4 %collective-permute-start.32 = (f32[2,512,128]{2,1,0:T(8,128)S(1)}, f32[2,512,128]{2,1,0:T(8,128)S(1)}, u32[]{:S(2)}, u32[]{:S(2)}) collective-permute-start(f32[2,512,128]{2,1,0:T(8,128)S(1)} %get-tuple-element.121.refs_2_), channel_id=1, source_target_pairs={{0,8},{8,0},{16,24},{24,16},{1,9},{9,1},{17,25},{25,17},{2,10},{10... | collective-permute-start | bytes 1572872 | tf_op jit(solution)/shard_map/ppermute | solution.py:559
  237.3 28.4 %collective-permute-start.33 = (f32[2,512,128]{2,1,0:T(8,128)S(1)}, f32[2,512,128]{2,1,0:T(8,128)S(1)}, u32[]{:S(2)}, u32[]{:S(2)}) collective-permute-start(f32[2,512,128]{2,1,0:T(8,128)S(1)} %get-tuple-element.122.refs_3_), channel_id=1, source_target_pairs={{0,8},{8,0},{16,24},{24,16},{1,9},{9,1},{17,25},{25,17},{2,10},{10... | collective-permute-start | bytes 1572872 | tf_op jit(solution)/shard_map/ppermute | solution.py:559
  260.7 52.1 %collective-permute-start.36 = (f32[2,512,128]{2,1,0:T(8,128)S(1)}, f32[2,512,128]{2,1,0:T(8,128)S(1)}, u32[]{:S(2)}, u32[]{:S(2)}) collective-permute-start(f32[2,512,128]{2,1,0:T(8,128)S(1)} %get-tuple-element.118.refs_0_), channel_id=1, source_target_pairs={{0,8},{8,0},{16,24},{24,16},{1,9},{9,1},{17,25},{25,17},{2,10},{10... | collective-permute-start | bytes 1572872 | tf_op jit(solution)/shard_map/ppermute | solution.py:559
  260.9 52.5 %collective-permute-start.37 = (f32[2,512,128]{2,1,0:T(8,128)S(1)}, f32[2,512,128]{2,1,0:T(8,128)}, u32[]{:S(2)}, u32[]{:S(2)}) collective-permute-start(f32[2,512,128]{2,1,0:T(8,128)S(1)} %get-tuple-element.128.refs_1_), channel_id=1, source_target_pairs={{0,8},{8,0},{16,24},{24,16},{1,9},{9,1},{17,25},{25,17},{2,10},{10... | collective-permute-start | bytes 1572872 | tf_op jit(solution)/shard_map/ppermute | solution.py:559
  261.3 60.6 %collective-permute-start.43 = (f32[2,4,128,256]{3,2,1,0:T(8,128)}, f32[2,4,128,256]{3,2,1,0:T(8,128)S(1)}, u32[]{:S(2)}, u32[]{:S(2)}) collective-permute-start(f32[2,4,128,256]{3,2,1,0:T(8,128)} %get-tuple-element.133), channel_id=1, source_target_pairs={{1,0},{2,1},{3,2},{4,3},{5,4},{6,5},{7,6},{9,8},{10,9},{11,10},{12... | collective-permute-start | bytes 3145736 | tf_op jit(solution)/shard_map/ppermute | solution.py:547
  265.8 47.7 %collective-permute-start.38 = (f32[2,512,128]{2,1,0:T(8,128)S(1)}, f32[2,512,128]{2,1,0:T(8,128)S(1)}, u32[]{:S(2)}, u32[]{:S(2)}) collective-permute-start(f32[2,512,128]{2,1,0:T(8,128)S(1)} %get-tuple-element.129.refs_2_), channel_id=1, source_target_pairs={{0,8},{8,0},{16,24},{24,16},{1,9},{9,1},{17,25},{25,17},{2,10},{10... | collective-permute-start | bytes 1572872 | tf_op jit(solution)/shard_map/ppermute | solution.py:559
  312.8 10.7 %collective-permute-start.44 = (f32[4,512,128]{2,1,0:T(8,128)S(1)}, f32[4,512,128]{2,1,0:T(8,128)S(1)}, u32[]{:S(2)}, u32[]{:S(2)}) collective-permute-start(f32[4,512,128]{2,1,0:T(8,128)S(1)} %get-tuple-element.126.refs_0_), channel_id=1, source_target_pairs={{0,8},{8,0},{16,24},{24,16},{1,9},{9,1},{17,25},{25,17},{2,10},{10... | collective-permute-start | bytes 3145736 | tf_op jit(solution)/shard_map/ppermute | solution.py:559
  314.6 48.7 %collective-permute-start.48 = (f32[2,2,128,1024]{3,2,1,0:T(8,128)}, f32[2,2,128,1024]{3,2,1,0:T(8,128)}, u32[]{:S(2)}, u32[]{:S(2)}) collective-permute-start(f32[2,2,128,1024]{3,2,1,0:T(8,128)} %mix.13.refs_5_), channel_id=1, source_target_pairs={{0,16},{8,24},{16,0},{24,8},{1,17},{9,25},{17,1},{25,9},{2,18},{10... | collective-permute-start | bytes 6291464 | tf_op jit(solution)/shard_map/ppermute | solution.py:570
  316.4 30.6 %collective-permute-start.45 = (f32[4,512,128]{2,1,0:T(8,128)S(1)}, f32[4,512,128]{2,1,0:T(8,128)}, u32[]{:S(2)}, u32[]{:S(2)}) collective-permute-start(f32[4,512,128]{2,1,0:T(8,128)S(1)} %get-tuple-element.136.refs_1_), channel_id=1, source_target_pairs={{0,8},{8,0},{16,24},{24,16},{1,9},{9,1},{17,25},{25,17},{2,10},{10... | collective-permute-start | bytes 3145736 | tf_op jit(solution)/shard_map/ppermute | solution.py:559
  321.9 86.4 %collective-permute-start.53 = (f32[2,2,128,1024]{3,2,1,0:T(8,128)}, f32[2,2,128,1024]{3,2,1,0:T(8,128)}, u32[]{:S(2)}, u32[]{:S(2)}) collective-permute-start(f32[2,2,128,1024]{3,2,1,0:T(8,128)} %mix.14.refs_6_), channel_id=1, source_target_pairs={{0,16},{8,24},{16,0},{24,8},{1,17},{9,25},{17,1},{25,9},{2,18},{10... | collective-permute-start | bytes 6291464 | tf_op jit(solution)/shard_map/ppermute | solution.py:570
  323.5 23.9 %collective-permute-start.46 = (f32[4,512,128]{2,1,0:T(8,128)S(1)}, f32[4,512,128]{2,1,0:T(8,128)S(1)}, u32[]{:S(2)}, u32[]{:S(2)}) collective-permute-start(f32[4,512,128]{2,1,0:T(8,128)S(1)} %get-tuple-element.137.refs_2_), channel_id=1, source_target_pairs={{0,8},{8,0},{16,24},{24,16},{1,9},{9,1},{17,25},{25,17},{2,10},{10... | collective-permute-start | bytes 3145736 | tf_op jit(solution)/shard_map/ppermute | solution.py:559
  323.5 24.1 %collective-permute-start.47 = (f32[4,512,128]{2,1,0:T(8,128)S(1)}, f32[4,512,128]{2,1,0:T(8,128)S(1)}, u32[]{:S(2)}, u32[]{:S(2)}) collective-permute-start(f32[4,512,128]{2,1,0:T(8,128)S(1)} %get-tuple-element.138.refs_3_), channel_id=1, source_target_pairs={{0,8},{8,0},{16,24},{24,16},{1,9},{9,1},{17,25},{25,17},{2,10},{10... | collective-permute-start | bytes 3145736 | tf_op jit(solution)/shard_map/ppermute | solution.py:559
  347.4 40.7 %collective-permute-start.50 = (f32[2,512,128]{2,1,0:T(8,128)S(1)}, f32[2,512,128]{2,1,0:T(8,128)}, u32[]{:S(2)}, u32[]{:S(2)}) collective-permute-start(f32[2,512,128]{2,1,0:T(8,128)S(1)} %get-tuple-element.143.refs_1_), channel_id=1, source_target_pairs={{0,8},{8,0},{16,24},{24,16},{1,9},{9,1},{17,25},{25,17},{2,10},{10... | collective-permute-start | bytes 1572872 | tf_op jit(solution)/shard_map/ppermute | solution.py:559
  347.6 40.6 %collective-permute-start.51 = (f32[2,512,128]{2,1,0:T(8,128)S(1)}, f32[2,512,128]{2,1,0:T(8,128)S(1)}, u32[]{:S(2)}, u32[]{:S(2)}) collective-permute-start(f32[2,512,128]{2,1,0:T(8,128)S(1)} %get-tuple-element.144.refs_2_), channel_id=1, source_target_pairs={{0,8},{8,0},{16,24},{24,16},{1,9},{9,1},{17,25},{25,17},{2,10},{10... | collective-permute-start | bytes 1572872 | tf_op jit(solution)/shard_map/ppermute | solution.py:559
  349.0 39.7 %collective-permute-start.52 = (f32[2,512,128]{2,1,0:T(8,128)S(1)}, f32[2,512,128]{2,1,0:T(8,128)S(1)}, u32[]{:S(2)}, u32[]{:S(2)}) collective-permute-start(f32[2,512,128]{2,1,0:T(8,128)S(1)} %get-tuple-element.145.refs_3_), channel_id=1, source_target_pairs={{0,8},{8,0},{16,24},{24,16},{1,9},{9,1},{17,25},{25,17},{2,10},{10... | collective-permute-start | bytes 1572872 | tf_op jit(solution)/shard_map/ppermute | solution.py:559
  363.4 67.4 %collective-permute-start.58 = (f32[2,4,128,256]{3,2,1,0:T(8,128)S(1)}, f32[2,4,128,256]{3,2,1,0:T(8,128)}, u32[]{:S(2)}, u32[]{:S(2)}) collective-permute-start(f32[2,4,128,256]{3,2,1,0:T(8,128)S(1)} %get-tuple-element.139.refs_7_), channel_id=1, source_target_pairs={{0,16},{8,24},{16,0},{24,8},{1,17},{9,25},{17,1},{25,9},{2,18},{10... | collective-permute-start | bytes 3145736 | tf_op jit(solution)/shard_map/ppermute | solution.py:600
  388.1 24.3 %collective-permute-start.54 = (f32[2,512,128]{2,1,0:T(8,128)S(1)}, f32[2,512,128]{2,1,0:T(8,128)S(1)}, u32[]{:S(2)}, u32[]{:S(2)}) collective-permute-start(f32[2,512,128]{2,1,0:T(8,128)S(1)} %get-tuple-element.141.refs_0_), channel_id=1, source_target_pairs={{0,8},{8,0},{16,24},{24,16},{1,9},{9,1},{17,25},{25,17},{2,10},{10... | collective-permute-start | bytes 1572872 | tf_op jit(solution)/shard_map/ppermute | solution.py:559
  388.2 25.8 %collective-permute-start.55 = (f32[2,512,128]{2,1,0:T(8,128)S(1)}, f32[2,512,128]{2,1,0:T(8,128)S(1)}, u32[]{:S(2)}, u32[]{:S(2)}) collective-permute-start(f32[2,512,128]{2,1,0:T(8,128)S(1)} %get-tuple-element.147.refs_1_), channel_id=1, source_target_pairs={{0,8},{8,0},{16,24},{24,16},{1,9},{9,1},{17,25},{25,17},{2,10},{10... | collective-permute-start | bytes 1572872 | tf_op jit(solution)/shard_map/ppermute | solution.py:559
  388.7 25.3 %collective-permute-start.56 = (f32[2,512,128]{2,1,0:T(8,128)S(1)}, f32[2,512,128]{2,1,0:T(8,128)S(1)}, u32[]{:S(2)}, u32[]{:S(2)}) collective-permute-start(f32[2,512,128]{2,1,0:T(8,128)S(1)} %get-tuple-element.148.refs_2_), channel_id=1, source_target_pairs={{0,8},{8,0},{16,24},{24,16},{1,9},{9,1},{17,25},{25,17},{2,10},{10... | collective-permute-start | bytes 1572872 | tf_op jit(solution)/shard_map/ppermute | solution.py:559
  412.4 40.8 %collective-permute-start.61 = (f32[2,4,128,256]{3,2,1,0:T(8,128)S(1)}, f32[2,4,128,256]{3,2,1,0:T(8,128)S(1)}, u32[]{:S(2)}, u32[]{:S(2)}) collective-permute-start(f32[2,4,128,256]{3,2,1,0:T(8,128)S(1)} %get-tuple-element.155.refs_7_), channel_id=1, source_target_pairs={{0,16},{8,24},{16,0},{24,8},{1,17},{9,25},{17,1},{25,9},{2,18},{10... | collective-permute-start | bytes 3145736 | tf_op jit(solution)/shard_map/ppermute | solution.py:600
  430.8 44.8 %collective-permute-start.59 = (f32[2,4,128,256]{3,2,1,0:T(8,128)S(1)}, f32[2,4,128,256]{3,2,1,0:T(8,128)S(1)}, u32[]{:S(2)}, u32[]{:S(2)}) collective-permute-start(f32[2,4,128,256]{3,2,1,0:T(8,128)S(1)} %get-tuple-element.152.refs_7_), channel_id=1, source_target_pairs={{0,16},{8,24},{16,0},{24,8},{1,17},{9,25},{17,1},{25,9},{2,18},{10... | collective-permute-start | bytes 3145736 | tf_op jit(solution)/shard_map/ppermute | solution.py:600
  453.1 43.2 %collective-permute-start.62 = (f32[2,4,128,128]{3,2,1,0:T(8,128)S(1)}, f32[2,4,128,128]{3,2,1,0:T(8,128)S(1)}, u32[]{:S(2)}, u32[]{:S(2)}) collective-permute-start(f32[2,4,128,128]{3,2,1,0:T(8,128)S(1)} %get-tuple-element.156.refs_7_), channel_id=1, source_target_pairs={{0,16},{8,24},{16,0},{24,8},{1,17},{9,25},{17,1},{25,9},{2,18},{10... | collective-permute-start | bytes 1572872 | tf_op jit(solution)/shard_map/ppermute | solution.py:600
  475.6 25.2 %collective-permute-start.60 = (f32[2,4,128,128]{3,2,1,0:T(8,128)S(1)}, f32[2,4,128,128]{3,2,1,0:T(8,128)S(1)}, u32[]{:S(2)}, u32[]{:S(2)}) collective-permute-start(f32[2,4,128,128]{3,2,1,0:T(8,128)S(1)} %get-tuple-element.153.refs_7_), channel_id=1, source_target_pairs={{0,16},{8,24},{16,0},{24,8},{1,17},{9,25},{17,1},{25,9},{2,18},{10... | collective-permute-start | bytes 1572872 | tf_op jit(solution)/shard_map/ppermute | solution.py:600
  (44 other events, 487.2 us)

commit v2 on v1

--- a/solution.py
+++ b/solution.py
@@ -22,11 +22,10 @@
 LANES = 128
 ROWS = 8
 HALF = ROWS // 2
-CUTS = 2
-PARTS = 2 * CUTS
 GROUP = 128
 LOW_BITS = 7
 VMEM_LIMIT = 48 * 1024 * 1024
+SERIES_FLOPS, SERIES_BYTES = 100_000_000, 300_000
 NO_COST = pl.CostEstimate(flops=1, bytes_accessed=1, transcendentals=0)
 
 
@@ -106,7 +105,9 @@
             jax.ShapeDtypeStruct((GROUP, GROUP), jnp.float32),
             jax.ShapeDtypeStruct((count, 8), jnp.float32),
         ],
-        cost_estimate=NO_COST,
+        cost_estimate=pl.CostEstimate(
+            flops=8_000_000_000, bytes_accessed=24_000_000, transcendentals=0
+        ),
         name="prepare",
     )(drive_bits, cosines, sines)
 
@@ -121,14 +122,15 @@
     frozen_coupling_ref,
     frozen_bits_ref,
     drive_ref,
+    matrix_ref,
     cutoff_ref,
     left_ref,
     middle_ref,
     right_ref,
     *refs,
 ):
-    out_refs = refs[:PARTS]
-    source, swapped, even_buffer, odd_buffer, ladder, diagonal = refs[PARTS:]
+    out_refs = refs[:-6]
+    source, swapped, even_buffer, odd_buffer, ladder, diagonal = refs[-6:]
     halo_tiles = left_ref.shape[3] // LANES
     own_tiles = middle_ref.shape[3] // LANES
     tiles = halo_tiles + own_tiles + halo_tiles
@@ -291,18 +293,35 @@
         if order > 0:
             fill_ghosts(target)
 
+    matrix = matrix_ref[...]
     for component in range(2):
         for half in range(halves):
-            for level in range(own_tiles * levels_per_tile):
-                start = start_of(component, half, level + halo_tiles * levels_per_tile)
-                out_ref = out_refs[component * CUTS + level * FB // out_refs[0].shape[1]]
-                first_row = level * FB % out_ref.shape[1]
-                out_ref[half, first_row : first_row + FB, :] = even_buffer[
-                    pl.ds(start, FB, stride=ROWS), :
-                ]
-
-
-def series_piece(scalars, cutoffs, sides, side_start, middle, first_group, groups, flip):
+            first_column = 0
+            for out_ref in out_refs:
+                for column in range(0, out_ref.shape[3], LANES):
+                    first = (first_column + column) // FB + halo_tiles * levels_per_tile
+                    evolved = jnp.concatenate(
+                        [
+                            even_buffer[
+                                pl.ds(start_of(component, half, level), FB, stride=ROWS), :
+                            ]
+                            for level in range(first, first + levels_per_tile)
+                        ],
+                        axis=0,
+                    )
+                    out_ref[component, half, :, column : column + LANES] = lax.dot_general(
+                        matrix,
+                        evolved,
+                        (((1,), (1,)), ((), ())),
+                        precision=lax.Precision.HIGHEST,
+                        preferred_element_type=jnp.float32,
+                    )
+                first_column += out_ref.shape[3]
+
+
+def series_piece(
+    scalars, matrix, cutoffs, sides, side_start, middle, first_group, groups, flip, widths
+):
     width = middle.shape[3]
     left, right = sides
     halo = left.shape[3]
@@ -316,13 +335,18 @@
         grid=(groups // halves,),
         in_specs=[SCALARS] * len(scalars)
         + [
+            pl.BlockSpec((GROUP, GROUP), lambda i: (0, 0)),
             pl.BlockSpec((1, GROUP * halves), lambda i: (0, i + first_unit)),
             pl.BlockSpec((2, halves, GROUP, halo), lambda i: (0, i + first_side, 0, 0)),
             pl.BlockSpec((2, halves, GROUP, width), lambda i: (0, i + first_unit, 0, 0)),
             pl.BlockSpec((2, halves, GROUP, halo), lambda i: (0, i + first_side, 0, 0)),
         ],
-        out_specs=[pl.BlockSpec((halves, width // CUTS, GROUP), lambda i: (i, 0, 0))] * PARTS,
-        out_shape=[jax.ShapeDtypeStruct((groups, width // CUTS, GROUP), jnp.float32)] * PARTS,
+        out_specs=[
+            pl.BlockSpec((2, halves, GROUP, chunk), lambda i: (0, i, 0, 0)) for chunk in widths
+        ],
+        out_shape=[
+            jax.ShapeDtypeStruct((2, groups, GROUP, chunk), jnp.float32) for chunk in widths
+        ],
         scratch_shapes=[
             field,
             field,
@@ -332,61 +356,21 @@
             pltpu.VMEM((depth * FB * ROWS, LANES), jnp.float32),
         ],
         compiler_params=pltpu.CompilerParams(vmem_limit_bytes=VMEM_LIMIT),
-        cost_estimate=NO_COST,
+        cost_estimate=pl.CostEstimate(
+            flops=groups * SERIES_FLOPS, bytes_accessed=groups * SERIES_BYTES, transcendentals=0
+        ),
         name="series",
-    )(*scalars, cutoffs, left, middle, right)
-
-
-def mix_kernel(spin, cosines, sines, matrix_ref, *refs):
-    own_refs, other_refs, out_refs = refs[:PARTS], refs[PARTS : 2 * PARTS], refs[2 * PARTS :]
-    side = (2 * (lax.axis_index("spin") & 1) - 1).astype(jnp.float32)
-    cosine = cosines[spin]
-    sine = side * sines[spin]
-    matrix = matrix_ref[...]
-    length = own_refs[0].shape[1]
-    for part in range(PARTS):
-        component, cut = divmod(part, CUTS)
-        mixed = lax.dot_general(
-            matrix,
-            cosine * own_refs[part][0] + sine * other_refs[part][0],
-            (((1,), (1,)), ((), ())),
-            precision=lax.Precision.HIGHEST,
-            preferred_element_type=jnp.float32,
-        )
-        start = 0
-        for out_ref in out_refs:
-            stop = start + out_ref.shape[3]
-            low, high = max(start, cut * length), min(stop, (cut + 1) * length)
-            if low < high:
-                out_ref[component, 0, :, low - start : high - start] = mixed[
-                    :, low - cut * length : high - cut * length
-                ]
-            start = stop
-
-
-def mix_piece(spin, cosines, sines, matrix, own, other, widths):
-    groups, length = own[0].shape[:2]
-    spec = pl.BlockSpec((1, length, GROUP), lambda i: (i, 0, 0))
-    return pl.pallas_call(
-        functools.partial(mix_kernel, spin),
-        grid=(groups,),
-        in_specs=[SCALARS, SCALARS, pl.BlockSpec((GROUP, GROUP), lambda i: (0, 0))]
-        + [spec] * (2 * PARTS),
-        out_specs=[pl.BlockSpec((2, 1, GROUP, width), lambda i: (0, i, 0, 0)) for width in widths],
-        out_shape=[jax.ShapeDtypeStruct((2, groups, GROUP, width), jnp.float32) for width in widths],
-        compiler_params=pltpu.CompilerParams(vmem_limit_bytes=VMEM_LIMIT),
-        cost_estimate=NO_COST,
-        name="mix",
-    )(cosines, sines, matrix, *own, *other)
-
-
-def join_kernel(counts, far_spin, cosines, sines, phase_ref, *refs):
+    )(*scalars, matrix, cutoffs, left, middle, right)
+
+
+def join_kernel(counts, core_spin, cosines, sines, phase_ref, *refs):
     pieces = len(counts)
     own_refs, other_refs, out_ref = refs[:pieces], refs[pieces : 2 * pieces], refs[-1]
     groups = sum(counts)
     bits = groups.bit_length() - 1
     width = out_ref.shape[3]
-    far_sine = (lax.axis_index("spin") & 2).astype(jnp.float32) * sines[far_spin] - sines[far_spin]
+    side = (2 * (lax.axis_index("spin") & 1) - 1).astype(jnp.float32)
+    core_sine = side * sines[core_spin]
     places = [(piece, index) for piece in range(pieces) for index in range(counts[piece])]
 
     def row_tile(step, carry):
@@ -396,8 +380,8 @@
             fields = []
             for component in range(2):
                 field = [
-                    cosines[far_spin] * own_refs[piece][component, index, rows, columns]
-                    + far_sine * other_refs[piece][component, index, rows, columns]
+                    cosines[core_spin] * own_refs[piece][component, index, rows, columns]
+                    + core_sine * other_refs[piece][component, index, rows, columns]
                     for piece, index in places
                 ]
                 for bit in range(bits):
@@ -423,7 +407,7 @@
     lax.fori_loop(0, out_ref.shape[2] // ROWS, row_tile, 0)
 
 
-def join_chunk(far_spin, cosines, sines, table, own, other, target, start, width, out_shape):
+def join_chunk(core_spin, cosines, sines, table, own, other, target, start, width, out_shape):
     counts = [piece.shape[1] for piece in own]
     groups = sum(counts)
     depth = GROUP // 2
@@ -446,7 +430,7 @@
         operands.append(target)
         in_specs.append(pl.BlockSpec(memory_space=pl.ANY))
     return pl.pallas_call(
-        functools.partial(join_kernel, counts, far_spin),
+        functools.partial(join_kernel, counts, core_spin),
         grid=(GROUP // depth,),
         in_specs=in_specs,
         out_specs=pl.BlockSpec((2, groups, depth, width), lambda i: (0, 0, i, chunk)),
@@ -472,21 +456,22 @@
 def piece_sizes(groups):
     if groups >= 16:
         unit = groups // 16
-        sizes = [2 * unit, unit, unit, 2 * unit, 2 * unit, 2 * unit, 2 * unit]
+        sizes = [4 * unit, unit, unit, 2 * unit, 2 * unit, 2 * unit]
     else:
-        sizes = [2, 1, 1]
+        sizes = [2, 2]
     return [*sizes, groups - sum(sizes)]
 
 
 def halo_batches(count):
-    batches = [1] * min(count, 4)
-    while sum(batches) < count:
-        batches.append(min(2, count - sum(batches)))
-    return batches
+    if count < 8:
+        return [2] + [1] * (count - 2)
+    return [2, 1, 2] + [1] * (count - 5)
 
 
 def chunk_widths(width):
     wide = 2 * LANES
+    if width > 2 * wide:
+        return [2 * wide] + [wide] * ((width - 3 * wide) // wide) + [LANES, LANES]
     return [wide] * (width // wide - 1) + [LANES, LANES]
 
 
@@ -526,22 +511,22 @@
     others = (coupling_second, frozen_coupling, frozen_bits, drive_bits)
 
     pieces = [(field, cutoffs, start, size, 0) for start, size in zip(starts, sizes)]
-    work = [*pieces[1:], (raw, raw_cutoffs, 0, raw_groups, 2), pieces[0]]
+    work = [*pieces, (raw, raw_cutoffs, 0, raw_groups, 2)][1:]
+    work.insert(-1, pieces[0])
     last = len(pieces) - 2
-    batches = halo_batches(last)
-    batches += [1, 2]
+    batches = halo_batches(len(work))
     halos = []
     sent = []
     evolved = []
-    crossed = []
-    own, other = [], []
+    other = []
 
     def send_halo(*earlier):
         batch = work[len(halos) : len(halos) + batches[len(sent)]]
         edges = []
         for low, high in ((width - halo, width), (0, halo)):
-            cuts = [source[:, start : start + size, :, low:high] for source, _, start, size, _ in batch]
-            edges.append(jnp.concatenate(cuts, axis=1) if len(cuts) > 1 else cuts[0])
+            source, _, start, _, _ = batch[0]
+            count = sum(piece[3] for piece in batch)
+            edges.append(source[:, start : start + count, :, low:high])
         if earlier:
             edges = lax.optimization_barrier((*edges, *earlier))[:2]
         sent.append((lax.ppermute(edges[0], "fock", up), lax.ppermute(edges[1], "fock", down)))
@@ -554,64 +539,57 @@
         index = len(evolved)
         source, cuts, start, size, flip = work[index]
         scalars = (tied(coupling_first, *earlier), *others)
-        piece = series_piece(scalars, cuts, *halos[index], source, start, size, flip)
+        widths = chunk_widths(width) if index == last else [width]
+        piece = series_piece(
+            scalars, matrix, cuts, *halos[index], source, start, size, flip, widths
+        )
         evolved.append(piece)
-        crossed.append([lax.ppermute(part, "spin", core_moves) for part in piece])
+        if index < last:
+            other.append(lax.ppermute(piece[0], "spin", far_moves))
         return piece[0]
 
-    def mix(index, *earlier):
-        widths = chunk_widths(width) if index == last else [width]
-        cosine = tied(cosines, *earlier)
-        mixed = mix_piece(
-            core_spin, cosine, sines, matrix, evolved[index], crossed[index], widths
-        )
-        if index < last:
-            own.append(mixed[0])
-            other.append(lax.ppermute(mixed[0], "spin", far_moves))
-        return mixed
+    far_sine = jnp.where(spin_place & 2 == 2, sines[far_spin], -sines[far_spin])
+
+    def far_rotated(piece, partner):
+        piece = cosines[far_spin] * piece + far_sine * partner
+        return piece, lax.ppermute(piece, "spin", core_moves)
 
     latest = matrix
+    landed = {last - 1: [0], last: [1], last + 1: [2], last + 2: [3]}
     send_halo()
-    prompt = min(4, last)
     for index in range(len(work)):
         waits = [latest]
-        if index == 2:
+        if index == min(3, last):
             waits.append(raw)
-        elif 2 < index < 6 and len(other) > index - 3:
-            waits.append(other[index - 3])
-        elif index > last and len(other) > index - 4:
-            waits.append(other[index - 4])
-        if len(sent) < len(batches):
-            send_halo(*halos[index][0])
+        waits += [other[place] for place in landed.get(index, []) if place < len(other)]
+        if index == 0 and len(sent) < len(batches):
+            send_halo(*sent[0])
         latest = series(*waits)
-        if index < prompt:
-            latest = mix(index, latest)[0]
-        elif prompt < index <= last + 1:
-            last_pieces = mix(index - 1, latest)
-            latest = last_pieces[0]
-    (raw_other,) = mix(last + 1, latest)
-    (raw_own,) = mix(last + 2, raw_other, other[-1])
-    own, other = [raw_own, *own], [raw_other, *other]
-    received = []
+        if index not in (1, 2) and len(sent) < len(batches):
+            send_halo(latest)
+    pairs = [far_rotated(evolved[last + 1][0], evolved[last + 2][0])]
+    pairs += [far_rotated(piece[0], partner) for piece, partner in zip(evolved, other)]
+    received = [lax.ppermute(piece, "spin", far_moves) for piece in evolved[last][:2]]
     result = None
     start = 0
-    for chunk, piece in enumerate(last_pieces):
-        going = piece if chunk < 2 else tied(piece, received[chunk - 2], raw_own)
-        received.append(lax.ppermute(going, "spin", far_moves))
-    for chunk, piece in enumerate(last_pieces):
+    for chunk, piece in enumerate(evolved[last]):
+        chunk_pairs = [*pairs, far_rotated(piece, received[chunk])]
         result = join_chunk(
-            far_spin,
+            core_spin,
             cosines,
             sines,
             phases,
-            [*own, piece],
-            [*other, received[chunk]],
+            [pair[0] for pair in chunk_pairs],
+            [pair[1] for pair in chunk_pairs],
             result,
             start,
             piece.shape[3],
             field.shape,
         )
         start += piece.shape[3]
+        if chunk + 2 < len(evolved[last]):
+            going, result = lax.optimization_barrier((evolved[last][chunk + 2], result))
+            received.append(lax.ppermute(going, "spin", far_moves))
     result = result.reshape(amplitudes.shape)
     for bit in range(2, spin_count.bit_length() - 1):
         spin = local_bits + bit

time: 513 us -> 565 us (1.10)
  Pallas kernels: 273 us -> 313 us
  starting transfers between devices: 71.4 us -> 49.2 us
  other arithmetic: 1.47 us -> 20.7 us
  local copies, waits for them, and re-layouts: 20.3 us -> 28.5 us
    pallas_call x9 -> x8, Pallas kernels: 208 us -> 283 us  [series_piece(): pl.pallas_call(functools.partial(series_kernel, series_weights(DEGREE), h...]
    ppermute x7 -> x6, waiting for transfers between devices: 36.6 us -> 76.5 us  [send_halo(): lax.ppermute(edges[1], 'fock', down)]
    ppermute x5 -> x2, waiting for transfers between devices: 50.6 us -> 14.9 us  [per_device(): received.append(lax.ppermute(going, 'spin', far_moves))]
    pallas_call x14 -> x4, Pallas kernels: 60.8 us -> 26.2 us  [join_chunk(): pl.pallas_call(functools.partial(join_kernel, counts, core_spin), grid=(G...]
    ppermute x1, waiting for transfers between devices: 0.01 us -> 31.5 us  [per_device(): lax.ppermute(cutoffs[:raw_groups * GROUP], 'spin', far_moves).reshape(1, -1)]
    ppermute x42 -> x17, waiting for transfers between devices: 40.7 us -> 17.8 us  [the longest x2 15 us: per_device(): lax.ppermute(piece, 'spin', far_moves)]
    add x0 -> x10, other arithmetic: none -> 20.7 us  [far_rotated(): piece = cosines[far_spin] * piece + far_sine * partner]
    ppermute x7 -> x6, waiting for transfers between devices: 10.8 us -> 0.02 us  [send_halo(): lax.ppermute(edges[0], 'fock', up)]
  transfers between devices with their start and end apart: 63 -> 33, of which waited for: 17 -> 8; matrix products, arithmetic and copies ran while one was open for 2% -> 6% of each run, Pallas kernels for 53% -> 56%
where the time goes in v2:
time: 565 us; the launch traced here: 555 us
  Pallas kernels  313 us (55%)
  waiting for transfers between devices  141 us (25%)
  starting transfers between devices  49.2 us (9%)
  local copies, waits for them, and re-layouts  28.5 us (5%)
  other arithmetic  20.7 us (4%)
    pallas_call x8, Pallas kernels, series_piece(): pl.pallas_call(functools.partial(series_kernel, series_weights(DEGREE), h...  283 us
    ppermute x6, waiting for transfers between devices, send_halo(): lax.ppermute(edges[1], 'fock', down)  76.5 us
    ppermute x1, waiting for transfers between devices, per_device(): lax.ppermute(cutoffs[:raw_groups * GROUP], 'spin', far_moves).reshape(1, -1)  31.5 us
    ppermute x6, starting transfers between devices, send_halo(): lax.ppermute(edges[1], 'fock', down)  29.4 us
    pallas_call x4, Pallas kernels, join_chunk(): pl.pallas_call(functools.partial(join_kernel, counts, core_spin), grid=(G...  26.2 us
    add x10, other arithmetic, far_rotated(): piece = cosines[far_spin] * piece + far_sine * partner  20.7 us
    ppermute x2, waiting for transfers between devices, per_device(): lax.ppermute(piece, 'spin', far_moves)  15 us
    ppermute x2, waiting for transfers between devices, per_device(): received.append(lax.ppermute(going, 'spin', far_moves))  14.9 us
  transfers between devices with their start and end apart: 33, of which 8 were waited for; matrix products, arithmetic and copies ran while one was open for 6% of the time, Pallas kernels for 56%

profile of v2, /device:TPU:26, one launch (start us, length us, event | category | flops | bytes accessed | tf_op | source)
XLA Modules:
  0.0 554.8 jit_solution(4814881446545835106)
XLA Ops:
  0.0 4.8 slice.78
  4.8 1.5 collective-permute-start.4
  6.3 1.7 fusion.1
  8.0 2.5 collective-permute-start.1
  10.5 1.3 collective-permute-start
  12.4 4.0 prepare.1
  16.4 16.2 %collective-permute-done.1.right_ref = f32[2,2,128,256]{3,2,1,0:T(8,128)S(1)} collective-permute-done((f32[2,2,128,256]{3,2,1,0:T(8,128)S(1)}, f32[2,2,128,256]{3,2,1,0:T(8,128)S(1)}, u32[]{:S(2)}, u32[]{:S(2)}) %collective-permute-start.1) | collective-permute-done | bytes 524320 | tf_op jit(solution)/shard_map/ppermute | solution.py:532
  32.6 1.4 collective-permute-start.2
  34.1 4.9 fusion
  39.0 15.6 %series.8 = f32[2,1,128,1024]{3,2,1,0:T(8,128)S(1)} custom-call(f32[13]{0:T(128)S(1)} %copy-done.19, f32[13]{0:T(128)S(1)} %copy-done.20, f32[16]{0:T(128)S(1)} %copy-done.21, s32[16]{0:T(128)S(1)} %copy-done.22, s32[13]{0:T(128)S(1)} %copy-done.18, f32[128,128]{1,0:T(8,128)S(1)} %copy-done.4, s32[1,2048]{1,0:T(1,128)S(1)} %bitcast.11, ...), custom_call_target="tpu_custom_call" | custom-call | flops 100000000 | bytes 300000 | tf_op jit(solution)/shard_map/series/pallas_call | solution.py:333
  54.6 1.3 collective-permute-start.5
  55.9 5.7 %collective-permute-start.6 = (f32[2,4,128,256]{3,2,1,0:T(8,128)S(1)}, f32[2,4,128,256]{3,2,1,0:T(8,128)S(1)}, u32[]{:S(2)}, u32[]{:S(2)}) collective-permute-start(f32[2,4,128,256]{3,2,1,0:T(8,128)S(1)} %get-tuple-element.42), channel_id=1, source_target_pairs={{1,0},{2,1},{3,2},{4,3},{5,4},{6,5},{7,6},{9,8},{10,9},{11,10},{12... | collective-permute-start | bytes 3145736 | tf_op jit(solution)/shard_map/ppermute | solution.py:532
  61.7 4.8 collective-permute-start.3
  67.0 15.8 %series.9 = f32[2,1,128,1024]{3,2,1,0:T(8,128)S(1)} custom-call(f32[13]{0:T(128)S(1)} %copy-done.19, f32[13]{0:T(128)S(1)} %copy-done.20, f32[16]{0:T(128)S(1)} %copy-done.21, s32[16]{0:T(128)S(1)} %copy-done.22, s32[13]{0:T(128)S(1)} %copy-done.18, f32[128,128]{1,0:T(8,128)S(1)} %copy-done.4, s32[1,2048]{1,0:T(1,128)S(1)} %bitcast.12, ...), custom_call_target="tpu_custom_call" | custom-call | flops 100000000 | bytes 300000 | tf_op jit(solution)/shard_map/series/pallas_call | solution.py:333
  82.9 33.7 %collective-permute-done.3.right_ref = f32[2,2,128,256]{3,2,1,0:T(8,128)S(1)} collective-permute-done((f32[2,2,128,256]{3,2,1,0:T(8,128)S(1)}, f32[2,2,128,256]{3,2,1,0:T(8,128)S(1)}, u32[]{:S(2)}, u32[]{:S(2)}) %collective-permute-start.3) | collective-permute-done | bytes 524320 | tf_op jit(solution)/shard_map/ppermute | solution.py:532
  116.6 26.9 %series.10 = f32[2,2,128,1024]{3,2,1,0:T(8,128)S(1)} custom-call(f32[13]{0:T(128)S(1)} %copy-done.19, f32[13]{0:T(128)S(1)} %copy-done.20, f32[16]{0:T(128)S(1)} %copy-done.21, s32[16]{0:T(128)S(1)} %copy-done.22, s32[13]{0:T(128)S(1)} %copy-done.18, f32[128,128]{1,0:T(8,128)S(1)} %copy-done.4, s32[1,2048]{1,0:T(1,128)S(1)} %bitcast.13, ...), custom_call_target="tpu_custom_call" | custom-call | flops 200000000 | bytes 600000 | tf_op jit(solution)/shard_map/series/pallas_call | solution.py:333
  144.0 1.5 collective-permute-start.8
  145.6 39.3 %series.11 = f32[2,2,128,1024]{3,2,1,0:T(8,128)S(1)} custom-call(f32[13]{0:T(128)S(1)} %copy-done.19, f32[13]{0:T(128)S(1)} %copy-done.20, f32[16]{0:T(128)S(1)} %copy-done.21, s32[16]{0:T(128)S(1)} %copy-done.22, s32[13]{0:T(128)S(1)} %copy-done.18, f32[128,128]{1,0:T(8,128)S(1)} %copy-done.4, s32[1,2048]{1,0:T(1,128)S(1)} %bitcast.14, ...), custom_call_target="tpu_custom_call" | custom-call | flops 200000000 | bytes 600000 | tf_op jit(solution)/shard_map/series/pallas_call | solution.py:333
  184.9 1.3 collective-permute-start.9
  186.2 5.1 collective-permute-start.10
  192.8 28.2 %series.12 = f32[2,2,128,1024]{3,2,1,0:T(8,128)} custom-call(f32[13]{0:T(128)S(1)} %copy-done.19, f32[13]{0:T(128)S(1)} %copy-done.20, f32[16]{0:T(128)S(1)} %copy-done.21, s32[16]{0:T(128)S(1)} %copy-done.22, s32[13]{0:T(128)S(1)} %copy-done.18, f32[128,128]{1,0:T(8,128)S(1)} %copy-done.4, s32[1,2048]{1,0:T(1,128)S(1)} %bitcast.15, ...), custom_call_target="tpu_custom_call" | custom-call | flops 200000000 | bytes 600000 | tf_op jit(solution)/shard_map/series/pallas_call | solution.py:333
  221.0 1.3 collective-permute-start.12
  222.3 5.4 collective-permute-start.13
  227.8 3.1 fusion.2
  230.9 26.6 %collective-permute-done.10.right_ref = f32[2,4,128,256]{3,2,1,0:T(8,128)S(1)} collective-permute-done((f32[2,4,128,256]{3,2,1,0:T(8,128)}, f32[2,4,128,256]{3,2,1,0:T(8,128)S(1)}, u32[]{:S(2)}, u32[]{:S(2)}) %collective-permute-start.10) | collective-permute-done | bytes 1048608 | tf_op jit(solution)/shard_map/ppermute | solution.py:532
  257.5 51.9 %series.13 = (f32[2,4,128,512]{3,2,1,0:T(8,128)}, f32[2,4,128,256]{3,2,1,0:T(8,128)S(1)}, f32[2,4,128,128]{3,2,1,0:T(8,128)S(1)}, f32[2,4,128,128]{3,2,1,0:T(8,128)S(1)}) custom-call(f32[13]{0:T(128)S(1)} %copy-done.19, f32[13]{0:T(128)S(1)} %copy-done.20, f32[16]{0:T(128)S(1)} %copy-done.21, s32[16]{0:T(128)S(1)} %copy-done.22, s32[13]{0:T(128)S(1)} %copy-done.18, ...), custom_call_target="tpu_custom_call" | custom-call | flops 400000000 | bytes 1200000 | tf_op jit(solution)/shard_map/series/pallas_call | solution.py:333
  312.1 1.3 collective-permute-start.16
  313.4 5.9 %collective-permute-start.17 = (f32[2,4,128,256]{3,2,1,0:T(8,128)}, f32[2,4,128,256]{3,2,1,0:T(8,128)}, u32[]{:S(2)}, u32[]{:S(2)}) collective-permute-start(f32[2,4,128,256]{3,2,1,0:T(8,128)} %get-tuple-element.53), channel_id=1, source_target_pairs={{1,0},{2,1},{3,2},{4,3},{5,4},{6,5},{7,6},{9,8},{10,9},{11,10},{12... | collective-permute-start | bytes 3145736 | tf_op jit(solution)/shard_map/ppermute | solution.py:532
  321.8 1.5 collective-permute-start.27
  328.9 52.5 %series.14 = f32[2,4,128,1024]{3,2,1,0:T(8,128)} custom-call(f32[13]{0:T(128)S(1)} %copy-done.19, f32[13]{0:T(128)S(1)} %copy-done.20, f32[16]{0:T(128)S(1)} %copy-done.21, s32[16]{0:T(128)S(1)} %copy-done.22, s32[13]{0:T(128)S(1)} %copy-done.18, f32[128,128]{1,0:T(8,128)S(1)} %copy-done.4, s32[1,2048]{1,0:T(1,128)S(1)} %bitcast.17, ...), custom_call_target="tpu_custom_call" | custom-call | flops 400000000 | bytes 1200000 | tf_op jit(solution)/shard_map/series/pallas_call | solution.py:333
  381.4 31.5 %collective-permute-done.15 = s32[512]{0:T(512)S(1)} collective-permute-done((s32[512]{0:T(512)S(1)}, s32[512]{0:T(512)S(1)}, u32[]{:S(2)}, u32[]{:S(2)}) %collective-permute-start.15) | collective-permute-done | bytes 2080 | tf_op jit(solution)/shard_map/ppermute | solution.py:506
  412.9 52.8 %series.15 = f32[2,4,128,1024]{3,2,1,0:T(8,128)} custom-call(f32[13]{0:T(128)S(1)} %copy-done.19, f32[13]{0:T(128)S(1)} %copy-done.20, f32[16]{0:T(128)S(1)} %copy-done.21, s32[16]{0:T(128)S(1)} %copy-done.22, s32[13]{0:T(128)S(1)} %copy-done.18, f32[128,128]{1,0:T(8,128)S(1)} %copy-done.4, s32[1,512]{1,0:T(1,128)S(1)} %bitcast.18, ...), custom_call_target="tpu_custom_call" | custom-call | flops 400000000 | bytes 1200000 | tf_op jit(solution)/shard_map/series/pallas_call | solution.py:333
  465.7 3.4 multiply_add_fusion.refs_0_
  469.3 3.9 multiply_add_fusion.6.refs_2_
  476.6 2.5 multiply_add_fusion.3.refs_4_
  479.1 4.1 multiply_add_fusion.2.refs_5_
  483.2 2.7 multiply_add_fusion.1.refs_6_
  486.6 15.0 %collective-permute-done.19 = f32[2,4,128,256]{3,2,1,0:T(8,128)S(1)} collective-permute-done((f32[2,4,128,256]{3,2,1,0:T(8,128)S(1)}, f32[2,4,128,256]{3,2,1,0:T(8,128)S(1)}, u32[]{:S(2)}, u32[]{:S(2)}) %collective-permute-start.19) | collective-permute-done | bytes 1048608 | tf_op jit(solution)/shard_map/ppermute | solution.py:572
  503.0 2.8 collective-permute-done.28.refs_13_
  505.8 1.3 copy-done.35
  507.1 1.3 copy-done.26
  508.5 11.2 %join.4.refs_14_ = f32[2,16,128,1024]{3,2,1,0:T(8,128)} custom-call(f32[13]{0:T(128)S(1)} %copy-done.24, f32[13]{0:T(128)S(1)} %copy-done.23, f32[16,128,8]{2,1,0:T(8,128)S(1)} %bitcast.7, f32[2,4,128,1024]{3,2,1,0:T(8,128)} %copy-done.25, f32[2,1,128,1024]{3,2,1,0:T(8,128)S(1)} %multiply_add_fusion.7.refs_1_, ...), custom_call_target="tpu_custom_call" | custom-call | flops 1 | bytes 1 | tf_op jit(solution)/shard_map/join/pallas_call | solution.py:432
  521.2 6.4 %join.5.refs_14_ = f32[2,16,128,1024]{3,2,1,0:T(8,128)} custom-call(f32[13]{0:T(128)S(1)} %copy-done.24, f32[13]{0:T(128)S(1)} %copy-done.23, f32[16,128,8]{2,1,0:T(8,128)S(1)} %bitcast.8, f32[2,4,128,1024]{3,2,1,0:T(8,128)} %copy-done.25, f32[2,1,128,1024]{3,2,1,0:T(8,128)S(1)} %multiply_add_fusion.7.refs_1_, ...), custom_call_target="tpu_custom_call", output_to_operand_aliasing={{}: (17, {})} | custom-call | flops 1 | bytes 1 | tf_op jit(solution)/shard_map/join/pallas_call | solution.py:432
  527.6 1.6 collective-permute-start.29
  529.2 5.3 collective-permute-done.31
  535.2 9.7 %collective-permute-done.29 = f32[2,4,128,128]{3,2,1,0:T(8,128)S(1)} collective-permute-done((f32[2,4,128,128]{3,2,1,0:T(8,128)S(1)}, f32[2,4,128,128]{3,2,1,0:T(8,128)S(1)}, u32[]{:S(2)}, u32[]{:S(2)}) %collective-permute-start.29) | collective-permute-done | bytes 524320 | tf_op jit(solution)/shard_map/ppermute | solution.py:592
  545.7 4.4 join.6.refs_14_
  550.0 4.4 join.7
  (135 shorter events, 21.3 us)
Async XLA Ops:
  4.8 7.0 %copy-start.42 = (f32[13]{0:T(128)S(1)}, f32[13]{0:T(128)}, u32[]{:S(2)}) copy-start(f32[13]{0:T(128)} %param.15) | copy-start | bytes 160
  4.8 139.2 %collective-permute-start.4 = (f32[2,4,128,1024]{3,2,1,0:T(8,128)}, f32[2,4,128,1024]{3,2,1,0:T(8,128)}, u32[]{:S(2)}, u32[]{:S(2)}) collective-permute-start(f32[2,4,128,1024]{3,2,1,0:T(8,128)} %slice.78), channel_id=1, source_target_pairs={{0,16},{8,24},{16,0},{24,8},{1,17},{9,25},{17,1},{25,9},{2,18},{10... | collective-permute-start | bytes 12582920 | tf_op jit(solution)/shard_map/ppermute | solution.py:505
  8.0 24.6 %collective-permute-start.1 = (f32[2,2,128,256]{3,2,1,0:T(8,128)S(1)}, f32[2,2,128,256]{3,2,1,0:T(8,128)S(1)}, u32[]{:S(2)}, u32[]{:S(2)}) collective-permute-start(f32[2,2,128,256]{3,2,1,0:T(8,128)S(1)} %get-tuple-element.69), channel_id=1, source_target_pairs={{1,0},{2,1},{3,2},{4,3},{5,4},{6,5},{7,6},{9,8},{10,9},{11,10},{12... | collective-permute-start | bytes 1572872 | tf_op jit(solution)/shard_map/ppermute | solution.py:532
  10.5 22.1 %collective-permute-start = (f32[2,2,128,256]{3,2,1,0:T(8,128)S(1)}, f32[2,2,128,256]{3,2,1,0:T(8,128)S(1)}, u32[]{:S(2)}, u32[]{:S(2)}) collective-permute-start(f32[2,2,128,256]{3,2,1,0:T(8,128)S(1)} %get-tuple-element.70), channel_id=1, source_target_pairs={{0,1},{1,2},{2,3},{3,4},{4,5},{5,6},{6,7},{8,9},{9,10},{10,11},{11... | collective-permute-start | bytes 1572872 | tf_op jit(solution)/shard_map/ppermute | solution.py:532
  32.6 6.4 %copy-start.18 = (s32[13]{0:T(128)S(1)}, s32[13]{0:T(128)}, u32[]{:S(2)}) copy-start(s32[13]{0:T(128)} %drive_ref.17) | copy-start | bytes 160
  32.6 6.4 %copy-start.19 = (f32[13]{0:T(128)S(1)}, f32[13]{0:T(128)}, u32[]{:S(2)}) copy-start(f32[13]{0:T(128)} %first_coupling_ref.7) | copy-start | bytes 160
  32.6 33.8 %collective-permute-start.2 = (f32[2,2,128,256]{3,2,1,0:T(8,128)S(1)}, f32[2,2,128,256]{3,2,1,0:T(8,128)S(1)}, u32[]{:S(2)}, u32[]{:S(2)}) collective-permute-start(f32[2,2,128,256]{3,2,1,0:T(8,128)S(1)} %get-tuple-element.38), channel_id=1, source_target_pairs={{0,1},{1,2},{2,3},{3,4},{4,5},{5,6},{6,7},{8,9},{9,10},{10,11},{11... | collective-permute-start | bytes 1572872 | tf_op jit(solution)/shard_map/ppermute | solution.py:532
  54.6 90.9 %collective-permute-start.5 = (f32[2,4,128,256]{3,2,1,0:T(8,128)S(1)}, f32[2,4,128,256]{3,2,1,0:T(8,128)S(1)}, u32[]{:S(2)}, u32[]{:S(2)}) collective-permute-start(f32[2,4,128,256]{3,2,1,0:T(8,128)S(1)} %get-tuple-element.41), channel_id=1, source_target_pairs={{0,1},{1,2},{2,3},{3,4},{4,5},{5,6},{6,7},{8,9},{9,10},{10,11},{11... | collective-permute-start | bytes 3145736 | tf_op jit(solution)/shard_map/ppermute | solution.py:532
  55.9 89.6 %collective-permute-start.6 = (f32[2,4,128,256]{3,2,1,0:T(8,128)S(1)}, f32[2,4,128,256]{3,2,1,0:T(8,128)S(1)}, u32[]{:S(2)}, u32[]{:S(2)}) collective-permute-start(f32[2,4,128,256]{3,2,1,0:T(8,128)S(1)} %get-tuple-element.42), channel_id=1, source_target_pairs={{1,0},{2,1},{3,2},{4,3},{5,4},{6,5},{7,6},{9,8},{10,9},{11,10},{12... | collective-permute-start | bytes 3145736 | tf_op jit(solution)/shard_map/ppermute | solution.py:532
  61.7 54.9 %collective-permute-start.3 = (f32[2,2,128,256]{3,2,1,0:T(8,128)S(1)}, f32[2,2,128,256]{3,2,1,0:T(8,128)S(1)}, u32[]{:S(2)}, u32[]{:S(2)}) collective-permute-start(f32[2,2,128,256]{3,2,1,0:T(8,128)S(1)} %get-tuple-element.39), channel_id=1, source_target_pairs={{1,0},{2,1},{3,2},{4,3},{5,4},{6,5},{7,6},{9,8},{10,9},{11,10},{12... | collective-permute-start | bytes 1572872 | tf_op jit(solution)/shard_map/ppermute | solution.py:532
  66.5 124.8 %collective-permute-start.7 = (f32[2,1,128,1024]{3,2,1,0:T(8,128)S(1)}, f32[2,1,128,1024]{3,2,1,0:T(8,128)S(1)}, u32[]{:S(2)}, u32[]{:S(2)}) collective-permute-start(f32[2,1,128,1024]{3,2,1,0:T(8,128)S(1)} %series.8), channel_id=1, source_target_pairs={{0,16},{8,24},{16,0},{24,8},{1,17},{9,25},{17,1},{25,9},{2,18},{10... | collective-permute-start | bytes 3145736 | tf_op jit(solution)/shard_map/ppermute | solution.py:548
  82.9 61.2 %copy-start.5 = (f32[2,1,128,1024]{3,2,1,0:T(8,128)}, f32[2,1,128,1024]{3,2,1,0:T(8,128)S(1)}, u32[]{:S(2)}) copy-start(f32[2,1,128,1024]{3,2,1,0:T(8,128)S(1)} %series.9) | copy-start | bytes 3145732
  143.5 41.4 %copy-start.2 = (f32[2,2,128,1024]{3,2,1,0:T(8,128)}, f32[2,2,128,1024]{3,2,1,0:T(8,128)S(1)}, u32[]{:S(2)}) copy-start(f32[2,2,128,1024]{3,2,1,0:T(8,128)S(1)} %series.10) | copy-start | bytes 6291460
  143.5 169.9 %collective-permute-start.11 = (f32[2,2,128,1024]{3,2,1,0:T(8,128)S(1)}, f32[2,2,128,1024]{3,2,1,0:T(8,128)S(1)}, u32[]{:S(2)}, u32[]{:S(2)}) collective-permute-start(f32[2,2,128,1024]{3,2,1,0:T(8,128)S(1)} %series.10), channel_id=1, source_target_pairs={{0,16},{8,24},{16,0},{24,8},{1,17},{9,25},{17,1},{25,9},{2,18},{10... | collective-permute-start | bytes 6291464 | tf_op jit(solution)/shard_map/ppermute | solution.py:548
  144.0 77.0 %collective-permute-start.8 = (f32[2,1,128,1024]{3,2,1,0:T(8,128)S(1)}, f32[2,1,128,1024]{3,2,1,0:T(8,128)}, u32[]{:S(2)}, u32[]{:S(2)}) collective-permute-start(f32[2,1,128,1024]{3,2,1,0:T(8,128)S(1)} %series.9), channel_id=1, source_target_pairs={{0,16},{8,24},{16,0},{24,8},{1,17},{9,25},{17,1},{25,9},{2,18},{10... | collective-permute-start | bytes 3145736 | tf_op jit(solution)/shard_map/ppermute | solution.py:548
  184.9 37.5 %collective-permute-start.9 = (f32[2,4,128,256]{3,2,1,0:T(8,128)}, f32[2,4,128,256]{3,2,1,0:T(8,128)S(1)}, u32[]{:S(2)}, u32[]{:S(2)}) collective-permute-start(f32[2,4,128,256]{3,2,1,0:T(8,128)} %get-tuple-element.45), channel_id=1, source_target_pairs={{0,1},{1,2},{2,3},{3,4},{4,5},{5,6},{6,7},{8,9},{9,10},{10,11},{11... | collective-permute-start | bytes 3145736 | tf_op jit(solution)/shard_map/ppermute | solution.py:532
  186.2 71.4 %collective-permute-start.10 = (f32[2,4,128,256]{3,2,1,0:T(8,128)}, f32[2,4,128,256]{3,2,1,0:T(8,128)S(1)}, u32[]{:S(2)}, u32[]{:S(2)}) collective-permute-start(f32[2,4,128,256]{3,2,1,0:T(8,128)} %get-tuple-element.46), channel_id=1, source_target_pairs={{1,0},{2,1},{3,2},{4,3},{5,4},{6,5},{7,6},{9,8},{10,9},{11,10},{12... | collective-permute-start | bytes 3145736 | tf_op jit(solution)/shard_map/ppermute | solution.py:532
  192.3 133.6 %collective-permute-start.14 = (f32[2,2,128,1024]{3,2,1,0:T(8,128)S(1)}, f32[2,2,128,1024]{3,2,1,0:T(8,128)}, u32[]{:S(2)}, u32[]{:S(2)}) collective-permute-start(f32[2,2,128,1024]{3,2,1,0:T(8,128)S(1)} %series.11), channel_id=1, source_target_pairs={{0,16},{8,24},{16,0},{24,8},{1,17},{9,25},{17,1},{25,9},{2,18},{10... | collective-permute-start | bytes 6291464 | tf_op jit(solution)/shard_map/ppermute | solution.py:548
  221.0 98.3 %collective-permute-start.12 = (f32[2,4,128,256]{3,2,1,0:T(8,128)}, f32[2,4,128,256]{3,2,1,0:T(8,128)S(1)}, u32[]{:S(2)}, u32[]{:S(2)}) collective-permute-start(f32[2,4,128,256]{3,2,1,0:T(8,128)} %get-tuple-element.49), channel_id=1, source_target_pairs={{0,1},{1,2},{2,3},{3,4},{4,5},{5,6},{6,7},{8,9},{9,10},{10,11},{11... | collective-permute-start | bytes 3145736 | tf_op jit(solution)/shard_map/ppermute | solution.py:532
  222.3 98.5 %collective-permute-start.13 = (f32[2,4,128,256]{3,2,1,0:T(8,128)S(1)}, f32[2,4,128,256]{3,2,1,0:T(8,128)S(1)}, u32[]{:S(2)}, u32[]{:S(2)}) collective-permute-start(f32[2,4,128,256]{3,2,1,0:T(8,128)S(1)} %get-tuple-element.50), channel_id=1, source_target_pairs={{1,0},{2,1},{3,2},{4,3},{5,4},{6,5},{7,6},{9,8},{10,9},{11,10},{12... | collective-permute-start | bytes 3145736 | tf_op jit(solution)/shard_map/ppermute | solution.py:532
  230.9 92.4 %copy-start.24 = (f32[13]{0:T(128)S(1)}, f32[13]{0:T(128)}, u32[]{:S(2)}) copy-start(f32[13]{0:T(128)} %get-tuple-element.74.cosines) | copy-start | bytes 160
  230.9 93.1 %copy-start.23 = (f32[13]{0:T(128)S(1)}, f32[13]{0:T(128)}, u32[]{:S(2)}) copy-start(f32[13]{0:T(128)} %get-tuple-element.73.sines) | copy-start | bytes 160
  312.1 100.8 %collective-permute-start.16 = (f32[2,4,128,256]{3,2,1,0:T(8,128)}, f32[2,4,128,256]{3,2,1,0:T(8,128)}, u32[]{:S(2)}, u32[]{:S(2)}) collective-permute-start(f32[2,4,128,256]{3,2,1,0:T(8,128)} %get-tuple-element.52), channel_id=1, source_target_pairs={{0,1},{1,2},{2,3},{3,4},{4,5},{5,6},{6,7},{8,9},{9,10},{10,11},{11... | collective-permute-start | bytes 3145736 | tf_op jit(solution)/shard_map/ppermute | solution.py:532
  313.4 7.4 %copy-start.36 = (f32[2,2,128,1024]{3,2,1,0:T(8,128)}, f32[2,2,128,1024]{3,2,1,0:T(8,128)S(1)}, u32[]{:S(2)}) copy-start(f32[2,2,128,1024]{3,2,1,0:T(8,128)S(1)} %collective-permute-done.11) | copy-start | bytes 6291460
  313.4 99.5 %collective-permute-start.17 = (f32[2,4,128,256]{3,2,1,0:T(8,128)}, f32[2,4,128,256]{3,2,1,0:T(8,128)}, u32[]{:S(2)}, u32[]{:S(2)}) collective-permute-start(f32[2,4,128,256]{3,2,1,0:T(8,128)} %get-tuple-element.53), channel_id=1, source_target_pairs={{1,0},{2,1},{3,2},{4,3},{5,4},{6,5},{7,6},{9,8},{10,9},{11,10},{12... | collective-permute-start | bytes 3145736 | tf_op jit(solution)/shard_map/ppermute | solution.py:532
  320.3 155.5 %collective-permute-start.18 = (f32[2,2,128,1024]{3,2,1,0:T(8,128)}, f32[2,2,128,1024]{3,2,1,0:T(8,128)}, u32[]{:S(2)}, u32[]{:S(2)}) collective-permute-start(f32[2,2,128,1024]{3,2,1,0:T(8,128)} %series.12), channel_id=1, source_target_pairs={{0,16},{8,24},{16,0},{24,8},{1,17},{9,25},{17,1},{25,9},{2,18},{10... | collective-permute-start | bytes 6291464 | tf_op jit(solution)/shard_map/ppermute | solution.py:548
  321.8 154.2 %collective-permute-start.27 = (f32[2,4,128,512]{3,2,1,0:T(8,128)}, f32[2,4,128,512]{3,2,1,0:T(8,128)}, u32[]{:S(2)}, u32[]{:S(2)}) collective-permute-start(f32[2,4,128,512]{3,2,1,0:T(8,128)} %get-tuple-element.47), channel_id=1, source_target_pairs={{0,16},{8,24},{16,0},{24,8},{1,17},{9,25},{17,1},{25,9},{2,18},{10... | collective-permute-start | bytes 6291464 | tf_op jit(solution)/shard_map/ppermute | solution.py:572
  325.9 87.0 %collective-permute-start.15 = (s32[512]{0:T(512)S(1)}, s32[512]{0:T(512)S(1)}, u32[]{:S(2)}, u32[]{:S(2)}) collective-permute-start(s32[512]{0:T(512)S(1)} %slice.71), channel_id=1, source_target_pairs={{0,16},{8,24},{16,0},{24,8},{1,17},{9,25},{17,1},{25,9},{2,18},{10... | collective-permute-start | bytes 6152 | tf_op jit(solution)/shard_map/ppermute | solution.py:506
  412.9 52.8 %copy-start.33 = (f32[2,4,128,1024]{3,2,1,0:T(8,128)S(1)}, f32[2,4,128,1024]{3,2,1,0:T(8,128)}, u32[]{:S(2)}) copy-start(f32[2,4,128,1024]{3,2,1,0:T(8,128)} %series.14) | copy-start | bytes 12582916
  469.2 36.5 %collective-permute-start.20 = (f32[2,4,128,1024]{3,2,1,0:T(8,128)S(1)}, f32[2,4,128,1024]{3,2,1,0:T(8,128)S(1)}, u32[]{:S(2)}, u32[]{:S(2)}) collective-permute-start(f32[2,4,128,1024]{3,2,1,0:T(8,128)S(1)} %multiply_add_fusion.refs_0_), channel_id=1, source_target_pairs={{0,8},{8,0},{16,24},{24,16},{1,9},{9,1},{17,25},{25,17},{2,10},{10... | collective-permute-start | bytes 12582920 | tf_op jit(solution)/shard_map/ppermute | solution.py:555
  473.2 12.8 %collective-permute-start.22 = (f32[2,1,128,1024]{3,2,1,0:T(8,128)S(1)}, f32[2,1,128,1024]{3,2,1,0:T(8,128)S(1)}, u32[]{:S(2)}, u32[]{:S(2)}) collective-permute-start(f32[2,1,128,1024]{3,2,1,0:T(8,128)S(1)} %multiply_add_fusion.6.refs_2_), channel_id=1, source_target_pairs={{0,8},{8,0},{16,24},{24,16},{1,9},{9,1},{17,25},{25,17},{2,10},{10... | collective-permute-start | bytes 3145736 | tf_op jit(solution)/shard_map/ppermute | solution.py:555
  474.2 12.0 %collective-permute-start.21 = (f32[2,1,128,1024]{3,2,1,0:T(8,128)S(1)}, f32[2,1,128,1024]{3,2,1,0:T(8,128)S(1)}, u32[]{:S(2)}, u32[]{:S(2)}) collective-permute-start(f32[2,1,128,1024]{3,2,1,0:T(8,128)S(1)} %multiply_add_fusion.7.refs_1_), channel_id=1, source_target_pairs={{0,8},{8,0},{16,24},{24,16},{1,9},{9,1},{17,25},{25,17},{2,10},{10... | collective-permute-start | bytes 3145736 | tf_op jit(solution)/shard_map/ppermute | solution.py:555
  475.9 26.5 %collective-permute-start.23 = (f32[2,2,128,1024]{3,2,1,0:T(8,128)S(1)}, f32[2,2,128,1024]{3,2,1,0:T(8,128)S(1)}, u32[]{:S(2)}, u32[]{:S(2)}) collective-permute-start(f32[2,2,128,1024]{3,2,1,0:T(8,128)S(1)} %multiply_add_fusion.4.refs_3_), channel_id=1, source_target_pairs={{0,8},{8,0},{16,24},{24,16},{1,9},{9,1},{17,25},{25,17},{2,10},{10... | collective-permute-start | bytes 6291464 | tf_op jit(solution)/shard_map/ppermute | solution.py:555
  476.1 25.5 %collective-permute-start.19 = (f32[2,4,128,256]{3,2,1,0:T(8,128)S(1)}, f32[2,4,128,256]{3,2,1,0:T(8,128)S(1)}, u32[]{:S(2)}, u32[]{:S(2)}) collective-permute-start(f32[2,4,128,256]{3,2,1,0:T(8,128)S(1)} %copy-done.12), channel_id=1, source_target_pairs={{0,16},{8,24},{16,0},{24,8},{1,17},{9,25},{17,1},{25,9},{2,18},{10... | collective-permute-start | bytes 3145736 | tf_op jit(solution)/shard_map/ppermute | solution.py:572
  479.1 7.1 %copy-start.28 = (f32[2,2,128,1024]{3,2,1,0:T(8,128)}, f32[2,2,128,1024]{3,2,1,0:T(8,128)S(1)}, u32[]{:S(2)}) copy-start(f32[2,2,128,1024]{3,2,1,0:T(8,128)S(1)} %multiply_add_fusion.3.refs_4_) | copy-start | bytes 6291460
  485.9 19.8 %copy-start.34 = (f32[2,4,128,512]{3,2,1,0:T(8,128)}, f32[2,4,128,512]{3,2,1,0:T(8,128)S(1)}, u32[]{:S(2)}) copy-start(f32[2,4,128,512]{3,2,1,0:T(8,128)S(1)} %multiply_add_fusion.1.refs_6_) | copy-start | bytes 6291460
  485.9 22.5 %copy-start = (f32[2048,8]{1,0:T(8,128)S(1)}, f32[2048,8]{1,0:T(8,128)}, u32[]{:S(2)}) copy-start(f32[2048,8]{1,0:T(8,128)} %get-tuple-element.33) | copy-start | bytes 196612
  486.0 33.6 %copy-start.1 = (f32[2,1,128,1024]{3,2,1,0:T(8,128)}, f32[2,1,128,1024]{3,2,1,0:T(8,128)S(1)}, u32[]{:S(2)}) copy-start(f32[2,1,128,1024]{3,2,1,0:T(8,128)S(1)} %collective-permute-done.22.refs_9_) | copy-start | bytes 3145732
  486.0 17.0 %collective-permute-start.25 = (f32[2,2,128,1024]{3,2,1,0:T(8,128)S(1)}, f32[2,2,128,1024]{3,2,1,0:T(8,128)S(1)}, u32[]{:S(2)}, u32[]{:S(2)}) collective-permute-start(f32[2,2,128,1024]{3,2,1,0:T(8,128)S(1)} %multiply_add_fusion.2.refs_5_), channel_id=1, source_target_pairs={{0,8},{8,0},{16,24},{24,16},{1,9},{9,1},{17,25},{25,17},{2,10},{10... | collective-permute-start | bytes 6291464 | tf_op jit(solution)/shard_map/ppermute | solution.py:555
  486.2 16.7 %collective-permute-start.24 = (f32[2,2,128,1024]{3,2,1,0:T(8,128)S(1)}, f32[2,2,128,1024]{3,2,1,0:T(8,128)S(1)}, u32[]{:S(2)}, u32[]{:S(2)}) collective-permute-start(f32[2,2,128,1024]{3,2,1,0:T(8,128)S(1)} %multiply_add_fusion.3.refs_4_), channel_id=1, source_target_pairs={{0,8},{8,0},{16,24},{24,16},{1,9},{9,1},{17,25},{25,17},{2,10},{10... | collective-permute-start | bytes 6291464 | tf_op jit(solution)/shard_map/ppermute | solution.py:555
  501.6 4.2 collective-permute-start.28
  502.4 17.8 %collective-permute-start.26 = (f32[2,4,128,256]{3,2,1,0:T(8,128)S(1)}, f32[2,4,128,256]{3,2,1,0:T(8,128)S(1)}, u32[]{:S(2)}, u32[]{:S(2)}) collective-permute-start(f32[2,4,128,256]{3,2,1,0:T(8,128)S(1)} %multiply_add_fusion.5.refs_6_), channel_id=1, source_target_pairs={{0,8},{8,0},{16,24},{24,16},{1,9},{9,1},{17,25},{25,17},{2,10},{10... | collective-permute-start | bytes 3145736 | tf_op jit(solution)/shard_map/ppermute | solution.py:555
  508.5 11.2 %copy-start.16 = (f32[2,4,128,128]{3,2,1,0:T(8,128)S(1)}, f32[2,4,128,128]{3,2,1,0:T(8,128)}, u32[]{:S(2)}) copy-start(f32[2,4,128,128]{3,2,1,0:T(8,128)} %copy-done.15) | copy-start | bytes 1572868
  519.6 8.0 %copy-start.14 = (f32[2,4,128,128]{3,2,1,0:T(8,128)S(1)}, f32[2,4,128,128]{3,2,1,0:T(8,128)}, u32[]{:S(2)}) copy-start(f32[2,4,128,128]{3,2,1,0:T(8,128)} %copy-done.13) | copy-start | bytes 1572868
  519.6 14.8 %collective-permute-start.31 = (f32[2,4,128,128]{3,2,1,0:T(8,128)S(1)}, f32[2,4,128,128]{3,2,1,0:T(8,128)S(1)}, u32[]{:S(2)}, u32[]{:S(2)}) collective-permute-start(f32[2,4,128,128]{3,2,1,0:T(8,128)S(1)} %copy-done.16), channel_id=1, source_target_pairs={{0,16},{8,24},{16,0},{24,8},{1,17},{9,25},{17,1},{25,9},{2,18},{10... | collective-permute-start | bytes 1572872 | tf_op jit(solution)/shard_map/ppermute | solution.py:592
  527.6 17.3 %collective-permute-start.29 = (f32[2,4,128,128]{3,2,1,0:T(8,128)S(1)}, f32[2,4,128,128]{3,2,1,0:T(8,128)S(1)}, u32[]{:S(2)}, u32[]{:S(2)}) collective-permute-start(f32[2,4,128,128]{3,2,1,0:T(8,128)S(1)} %copy-done.14), channel_id=1, source_target_pairs={{0,16},{8,24},{16,0},{24,8},{1,17},{9,25},{17,1},{25,9},{2,18},{10... | collective-permute-start | bytes 1572872 | tf_op jit(solution)/shard_map/ppermute | solution.py:592
  535.2 10.5 %collective-permute-start.32 = (f32[2,4,128,128]{3,2,1,0:T(8,128)S(1)}, f32[2,4,128,128]{3,2,1,0:T(8,128)S(1)}, u32[]{:S(2)}, u32[]{:S(2)}) collective-permute-start(f32[2,4,128,128]{3,2,1,0:T(8,128)S(1)} %multiply_add_fusion.8.refs_6_), channel_id=1, source_target_pairs={{0,8},{8,0},{16,24},{24,16},{1,9},{9,1},{17,25},{25,17},{2,10},{10... | collective-permute-start | bytes 1572872 | tf_op jit(solution)/shard_map/ppermute | solution.py:555
  545.6 4.5 collective-permute-start.30
  (28 other events, 85.9 us)
